TPU v7x, 32 devices: a whole 2x2x4 slice. The times are simulated.
32 devices in a mesh: groups: 2 (over x), ex: 16 (over z, y, core).
Axes of the slice: x: 2, y: 2, z: 4, core: 2. Of those that a mesh axis runs over, the one named last changes fastest.
Arguments:
- acts: bfloat16 [24576, 5120], P(('groups', 'ex')), parts along dimension 0, may hold values from -6 to 6
- grads: bfloat16 [24576, 1024], P(('groups', 'ex')), parts along dimension 0, may hold values from -6 to 6
- domain: int32 [3072], P(('groups', 'ex')), parts along dimension 0, may hold values from 0 to 47
- listed: int32 [32, 2], P(('groups', 'ex')), parts along dimension 0, may hold values 0 or 1
Outputs:
- influence: float32 [3072, 48], P(('groups', 'ex')), parts along dimension 0
There are 2 independent parts, one for each index of `groups`. A program takes and returns all parts, laid end to end along the dimension named above; each array names one. Nothing has to cross between parts.
All inputs are finite; a program needn't handle non-finite values. No bound on the sum of `listed` on one device may be relied on, other than what follows from the above.
Results may differ from a plain program's by a relative error of at most 0.0003.
Values may be sent and summed in bfloat16 or wider, within the bound.
No kernel may reach another device: no remote copies, remote signals or barrier semaphores. Data moves between devices by JAX's collectives and lax.ppermute only.
A program may use at most 192 MiB of HBM per device.

v0:
```python
import math

import jax
import jax.numpy as jnp
from jax import lax
from jax.sharding import PartitionSpec as P

TOK = 8
DOMAINS = 48
REACH = 2


def from_behind(value, axis, steps):
    count = lax.axis_size(axis)
    pairs = [(source, (source + steps) % count) for source in range(count)]
    return lax.ppermute(value, axis, pairs)


def pair_scores(acts_one, grads_one, acts_two, grads_two):
    contract = (((1,), (1,)), ((), ()))
    inner_acts = lax.dot_general(acts_one, acts_two, contract, preferred_element_type=jnp.float32)
    inner_grads = lax.dot_general(
        grads_one, grads_two, contract, preferred_element_type=jnp.float32
    )
    per_block = acts_one.shape[0] // TOK
    factor = 1.0 / (TOK * math.sqrt(acts_one.shape[1] * grads_one.shape[1]))
    return (inner_acts * inner_grads).reshape(per_block, TOK, per_block, TOK).sum(
        axis=(1, 3)
    ) * factor


def listed_scores(listed_flag, acts_one, grads_one, acts_two, grads_two):
    return pair_scores(acts_one, grads_one, acts_two, grads_two) * listed_flag.astype(jnp.float32)


def make_hot(labels):
    return (labels[:, None] == jnp.arange(DOMAINS, dtype=jnp.int32)[None, :]).astype(jnp.float32)


def domain_sums(scores, hot_table):
    return jnp.dot(scores, hot_table, precision=lax.Precision.HIGHEST)


def per_device(acts, grads, domain, listed):
    own_hot = make_hot(domain)
    carried = (acts, grads, domain)
    total = jnp.zeros(own_hot.shape, jnp.float32)
    for offset in range(REACH):
        carried = from_behind((carried[0], carried[1], carried[2]), "ex", -1)
        scores = listed_scores(listed[0, offset], acts, grads, carried[0], carried[1])
        total = total + domain_sums(scores, make_hot(carried[2]))
        back_part = domain_sums(scores.T, own_hot)
        total = total + from_behind(back_part, "ex", offset + 1)
    return total


def solution(mesh):
    in_specs = (
        P(("groups", "ex"), None),
        P(("groups", "ex"), None),
        P(("groups", "ex")),
        P(("groups", "ex"), None),
    )
    out_specs = P(("groups", "ex"), None)
    return jax.shard_map(
        per_device, mesh=mesh, in_specs=in_specs, out_specs=out_specs, check_vma=False
    )
```

profile of v0, /device:TPU:0, one launch (start us, length us, event | category | flops | bytes accessed | tf_op | source)
XLA Modules:
  0.0 333.4 jit_solution(14294006358955049120)
XLA Ops:
  0.0 5.4 %collective-permute-start = (bf16[768,5120]{1,0:T(8,128)(2,1)}, bf16[768,5120]{1,0:T(8,128)(2,1)}, u32[]{:S(2)}, u32[]{:S(2)}) collective-permute-start(bf16[768,5120]{1,0:T(8,128)(2,1)} %param.4), channel_id=1, source_target_pairs={{0,15},{1,0},{2,1},{3,2},{4,3},{5,4},{6,5},{7,6},{8,7},{9,8},{10,9... | collective-permute-start | bytes 23592968 | tf_op jit(solution)/shard_map/ppermute | solution.py:16
  5.4 85.7 %collective-permute-done = bf16[768,5120]{1,0:T(8,128)(2,1)} collective-permute-done((bf16[768,5120]{1,0:T(8,128)(2,1)}, bf16[768,5120]{1,0:T(8,128)(2,1)}, u32[]{:S(2)}, u32[]{:S(2)}) %collective-permute-start) | collective-permute-done | bytes 7864352 | tf_op jit(solution)/shard_map/ppermute | solution.py:16
  91.1 4.6 %collective-permute-start.4 = (bf16[768,5120]{1,0:T(8,128)(2,1)}, bf16[768,5120]{1,0:T(8,128)(2,1)}, u32[]{:S(2)}, u32[]{:S(2)}) collective-permute-start(bf16[768,5120]{1,0:T(8,128)(2,1)} %collective-permute-done), channel_id=1, source_target_pairs={{0,15},{1,0},{2,1},{3,2},{4,3},{5,4},{6,5},{7,6},{8,7},{9,8},{10,9... | collective-permute-start | bytes 23592968 | tf_op jit(solution)/shard_map/ppermute | solution.py:16
  95.7 0.0 collective-permute-start.1
  95.7 102.5 %collective-permute-done.1 = bf16[768,1024]{1,0:T(8,128)(2,1)S(1)} collective-permute-done((bf16[768,1024]{1,0:T(8,128)(2,1)}, bf16[768,1024]{1,0:T(8,128)(2,1)S(1)}, u32[]{:S(2)}, u32[]{:S(2)}) %collective-permute-start.1) | collective-permute-done | bytes 1572896 | tf_op jit(solution)/shard_map/ppermute | solution.py:16
  198.2 4.5 %collective-permute-start.5 = (bf16[768,1024]{1,0:T(8,128)(2,1)S(1)}, bf16[768,1024]{1,0:T(8,128)(2,1)S(1)}, u32[]{:S(2)}, u32[]{:S(2)}) collective-permute-start(bf16[768,1024]{1,0:T(8,128)(2,1)S(1)} %collective-permute-done.1), channel_id=1, source_target_pairs={{0,15},{1,0},{2,1},{3,2},{4,3},{5,4},{6,5},{7,6},{8,7},{9,8},{10,9... | collective-permute-start | bytes 4718600 | tf_op jit(solution)/shard_map/ppermute | solution.py:16
  202.8 1.4 fusion.15
  205.4 15.3 %collective-permute-done.2 = s32[96]{0:T(128)S(1)} collective-permute-done((s32[96]{0:T(128)}, s32[96]{0:T(128)S(1)}, u32[]{:S(2)}, u32[]{:S(2)}) %collective-permute-start.2) | collective-permute-done | bytes 416 | tf_op jit(solution)/shard_map/ppermute | solution.py:16
  220.7 4.6 %collective-permute-start.6 = (s32[96]{0:T(128)S(1)}, s32[96]{0:T(128)S(1)}, u32[]{:S(2)}, u32[]{:S(2)}) collective-permute-start(s32[96]{0:T(128)S(1)} %collective-permute-done.2), channel_id=1, source_target_pairs={{0,15},{1,0},{2,1},{3,2},{4,3},{5,4},{6,5},{7,6},{8,7},{9,8},{10,9... | collective-permute-start | bytes 1160 | tf_op jit(solution)/shard_map/ppermute | solution.py:16
  225.3 3.0 fusion.16
  228.3 2.8 fusion.17
  231.2 8.9 %convolution_multiply_fusion.1 = f32[768,768]{1,0:T(8,128)S(1)} fusion(f32[768,768]{1,0:T(8,128)S(1)} %fusion.16, bf16[768,5120]{1,0:T(8,128)(2,1)S(1)} %bitcast.11, bf16[768,5120]{1,0:T(8,128)(2,1)} %collective-permute-done), kind=kOutput, calls=%fused_computation.1 | convolution fusion | flops 6040387584 | bytes 20447232 | tf_op jit(solution)/shard_map/dot_general | solution.py:21
  240.1 23.1 %reshape.15 = f32[96,8,96,8]{3,2,1,0:T(8,128)} reshape(f32[768,768]{1,0:T(8,128)S(1)} %convolution_multiply_fusion.1) | data formatting | bytes 4718592 | tf_op jit(solution)/shard_map/reshape | solution.py:27
  263.2 13.8 %reduce_sum.18 = f32[96,96]{1,0:T(8,128)S(1)} reduce(f32[96,8,96,8]{3,2,1,0:T(8,128)} %reshape.15, f32[]{:T(128)} %constant.4.clone.1), dimensions={1,3}, to_apply=%region_0.0 | reduce | flops 580608 | bytes 2396164 | tf_op jit(solution)/shard_map/reduce_sum | solution.py:27
  277.0 0.3 fusion.2
  277.3 0.1 collective-permute-start.3
  277.4 11.3 %convolution_multiply_fusion = f32[768,768]{1,0:T(8,128)S(1)} fusion(f32[768,768]{1,0:T(8,128)} %fusion.17, bf16[768,5120]{1,0:T(8,128)(2,1)} %param.4, bf16[768,5120]{1,0:T(8,128)(2,1)} %collective-permute-done.4), kind=kOutput, calls=%fused_computation | convolution fusion | flops 6040387584 | bytes 20447232 | tf_op jit(solution)/shard_map/dot_general | solution.py:21
  288.7 23.1 %reshape.16 = f32[96,8,96,8]{3,2,1,0:T(8,128)} reshape(f32[768,768]{1,0:T(8,128)S(1)} %convolution_multiply_fusion) | data formatting | bytes 4718592 | tf_op jit(solution)/shard_map/reshape | solution.py:27
  311.8 13.8 %reduce_sum.19 = f32[96,96]{1,0:T(8,128)S(1)} reduce(f32[96,8,96,8]{3,2,1,0:T(8,128)} %reshape.16, f32[]{:T(128)} %constant.4.clone.1), dimensions={1,3}, to_apply=%region_1.0 | reduce | flops 580608 | bytes 2396164 | tf_op jit(solution)/shard_map/reduce_sum | solution.py:27
  325.6 0.3 fusion.1
  325.9 0.1 collective-permute-start.7
  326.0 0.3 convolution_add_fusion.1
  326.3 6.2 %collective-permute-done.7 = f32[96,48]{0,1:T(8,128)S(1)} collective-permute-done((f32[96,48]{0,1:T(8,128)S(1)}, f32[96,48]{0,1:T(8,128)S(1)}, u32[]{:S(2)}, u32[]{:S(2)}) %collective-permute-start.7) | collective-permute-done | bytes 18464 | tf_op jit(solution)/shard_map/ppermute | solution.py:16
  332.5 0.9 fusion
  (14 shorter events, 0.1 us)
Async XLA Ops:
  0.0 91.1 %collective-permute-start = (bf16[768,5120]{1,0:T(8,128)(2,1)}, bf16[768,5120]{1,0:T(8,128)(2,1)}, u32[]{:S(2)}, u32[]{:S(2)}) collective-permute-start(bf16[768,5120]{1,0:T(8,128)(2,1)} %param.4), channel_id=1, source_target_pairs={{0,15},{1,0},{2,1},{3,2},{4,3},{5,4},{6,5},{7,6},{8,7},{9,8},{10,9... | collective-permute-start | bytes 23592968 | tf_op jit(solution)/shard_map/ppermute | solution.py:16
  91.1 186.3 %collective-permute-start.4 = (bf16[768,5120]{1,0:T(8,128)(2,1)}, bf16[768,5120]{1,0:T(8,128)(2,1)}, u32[]{:S(2)}, u32[]{:S(2)}) collective-permute-start(bf16[768,5120]{1,0:T(8,128)(2,1)} %collective-permute-done), channel_id=1, source_target_pairs={{0,15},{1,0},{2,1},{3,2},{4,3},{5,4},{6,5},{7,6},{8,7},{9,8},{10,9... | collective-permute-start | bytes 23592968 | tf_op jit(solution)/shard_map/ppermute | solution.py:16
  95.7 102.5 %collective-permute-start.1 = (bf16[768,1024]{1,0:T(8,128)(2,1)}, bf16[768,1024]{1,0:T(8,128)(2,1)S(1)}, u32[]{:S(2)}, u32[]{:S(2)}) collective-permute-start(bf16[768,1024]{1,0:T(8,128)(2,1)} %param.5), channel_id=1, source_target_pairs={{0,15},{1,0},{2,1},{3,2},{4,3},{5,4},{6,5},{7,6},{8,7},{9,8},{10,9... | collective-permute-start | bytes 4718600 | tf_op jit(solution)/shard_map/ppermute | solution.py:16
  198.2 30.1 %collective-permute-start.5 = (bf16[768,1024]{1,0:T(8,128)(2,1)S(1)}, bf16[768,1024]{1,0:T(8,128)(2,1)S(1)}, u32[]{:S(2)}, u32[]{:S(2)}) collective-permute-start(bf16[768,1024]{1,0:T(8,128)(2,1)S(1)} %collective-permute-done.1), channel_id=1, source_target_pairs={{0,15},{1,0},{2,1},{3,2},{4,3},{5,4},{6,5},{7,6},{8,7},{9,8},{10,9... | collective-permute-start | bytes 4718600 | tf_op jit(solution)/shard_map/ppermute | solution.py:16
  202.7 18.0 %collective-permute-start.2 = (s32[96]{0:T(128)}, s32[96]{0:T(128)S(1)}, u32[]{:S(2)}, u32[]{:S(2)}) collective-permute-start(s32[96]{0:T(128)} %param.6), channel_id=1, source_target_pairs={{0,15},{1,0},{2,1},{3,2},{4,3},{5,4},{6,5},{7,6},{8,7},{9,8},{10,9... | collective-permute-start | bytes 1160 | tf_op jit(solution)/shard_map/ppermute | solution.py:16
  205.4 22.9 %copy-start = (bf16[768,1024]{1,0:T(8,128)(2,1)S(1)}, bf16[768,1024]{1,0:T(8,128)(2,1)}, u32[]{:S(2)}) copy-start(bf16[768,1024]{1,0:T(8,128)(2,1)} %param.5) | copy-start | bytes 4718596
  220.7 105.6 %collective-permute-start.6 = (s32[96]{0:T(128)S(1)}, s32[96]{0:T(128)S(1)}, u32[]{:S(2)}, u32[]{:S(2)}) collective-permute-start(s32[96]{0:T(128)S(1)} %collective-permute-done.2), channel_id=1, source_target_pairs={{0,15},{1,0},{2,1},{3,2},{4,3},{5,4},{6,5},{7,6},{8,7},{9,8},{10,9... | collective-permute-start | bytes 1160 | tf_op jit(solution)/shard_map/ppermute | solution.py:16
  225.3 5.9 %slice-start = ((s8[7864320]{0:T(1024)(128)(4,1)}), s8[4194304]{0:T(1024)(128)(4,1)S(1)}, s32[]{:S(2)}) async-start(s8[7864320]{0:T(1024)(128)(4,1)} %bitcast.10), calls=%async_computation | async-start | bytes 8388608
  228.3 2.9 slice-start.1
  263.2 13.8 %copy-start.1 = (s32[96]{0:T(128)S(1)}, s32[96]{0:T(128)}, u32[]{:S(2)}) copy-start(s32[96]{0:T(128)} %param.6) | copy-start | bytes 1156
  277.3 48.6 %collective-permute-start.3 = (f32[96,48]{0,1:T(8,128)S(1)}, f32[96,48]{0,1:T(8,128)S(1)}, u32[]{:S(2)}, u32[]{:S(2)}) collective-permute-start(f32[96,48]{0,1:T(8,128)S(1)} %fusion.2), channel_id=1, source_target_pairs={{0,1},{1,2},{2,3},{3,4},{4,5},{5,6},{6,7},{7,8},{8,9},{9,10},{10,1... | collective-permute-start | bytes 55304 | tf_op jit(solution)/shard_map/ppermute | solution.py:16
  325.9 6.6 %collective-permute-start.7 = (f32[96,48]{0,1:T(8,128)S(1)}, f32[96,48]{0,1:T(8,128)S(1)}, u32[]{:S(2)}, u32[]{:S(2)}) collective-permute-start(f32[96,48]{0,1:T(8,128)S(1)} %fusion.1), channel_id=1, source_target_pairs={{0,2},{1,3},{2,4},{3,5},{4,6},{5,7},{6,8},{7,9},{8,10},{9,11},{10,... | collective-permute-start | bytes 55304 | tf_op jit(solution)/shard_map/ppermute | solution.py:16
where the time goes:
time: 334 us; the launch traced here: 333 us
  waiting for transfers between devices  210 us (63%)
  local copies, waits for them, and re-layouts  47.6 us (14%)
  matrix products  27.8 us (8%)
  other arithmetic  27.6 us (8%)
  starting transfers between devices  19.4 us (6%)
    ppermute x8, waiting for transfers between devices, from_behind(): return lax.ppermute(value, axis, pairs)  210 us
    reshape x2, local copies, waits for them, and re-layouts, pair_scores(): (inner_acts * inner_grads).reshape(per_block, TOK, per_block, TOK)  46.2 us
    reduce_sum x2, other arithmetic, pair_scores(): (inner_acts * inner_grads).reshape(per_block, TOK, per_block, TOK)  27.6 us
    dot_general x2, matrix products, pair_scores(): lax.dot_general(acts_one, acts_two, contract, preferred_element_type=jnp....  20.2 us
    ppermute x8, starting transfers between devices, from_behind(): return lax.ppermute(value, axis, pairs)  19.4 us
  transfers between devices with their start and end apart: 8, of which 4 were waited for; matrix products, arithmetic and copies ran while one was open for 31% of the time, Pallas kernels for 0%

commit v1 on v0

v1 whole, which is shorter than its diff:
```python
import functools
import math

import jax
import jax.numpy as jnp
from jax import lax
from jax.experimental import pallas as pl
from jax.experimental.pallas import tpu as pltpu
from jax.sharding import PartitionSpec as P

TOK = 8
DOMAINS = 48
LANES = 128
VMEM_BYTES = 56 * 1024 * 1024

XS, XC, YS, YC, ZS, ZC = range(6)
PAIRS = (
    (XS, YS, 1), (YS, ZS, 1), (XC, YS, 0), (XS, XC, 0),
    (XC, YC, 1), (YC, ZC, 1), (YC, ZS, 0), (YS, ZC, 0), (XS, YC, 0),
)
ONLY = {2: 0, 6: 0, 7: 1, 8: 1}
SLOT = (0, 1, 2, 3, 4, 5, 6, 6, 2)
FIRST = (0, 1, 2, 3)
SECOND = (4, 5, 6, 7, 8)
NT = (((1,), (1,)), ((), ()))


def across(chip):
    return chip ^ 1


def along(chip):
    return chip + 2 if chip & 1 else chip - 2


def against(chip):
    return chip - 2 if chip & 1 else chip + 2


def stay(chip):
    return chip


def send(value, move, flip):
    chips = lax.axis_size("ex") // 2
    pairs = [
        (2 * chip + core, 2 * (move(chip) % chips) + (core ^ flip))
        for chip in range(chips)
        for core in range(2)
    ]
    return lax.ppermute(value, "ex", pairs)


def cut_kernel(offsets, acts, y_same, z_same, x_half, y_cross, z_cross, sems):
    copies = []
    for at, out in enumerate((y_same, z_same, x_half, y_cross, z_cross)):
        start = pl.multiple_of(offsets[at], LANES)
        copies.append(pltpu.make_async_copy(acts.at[:, pl.ds(start, out.shape[1])], out, sems.at[at]))
    for copy in copies:
        copy.start()
    for copy in copies:
        copy.wait()


def cut(acts, offsets):
    rows, width = acts.shape
    quarter = width // 4
    widths = (quarter, quarter, 2 * quarter, quarter, quarter)
    return pl.pallas_call(
        cut_kernel,
        in_specs=[pl.BlockSpec(memory_space=pltpu.SMEM), pl.BlockSpec(memory_space=pl.ANY)],
        out_specs=[pl.BlockSpec(memory_space=pl.ANY)] * 5,
        out_shape=[jax.ShapeDtypeStruct((rows, w), acts.dtype) for w in widths],
        scratch_shapes=[pltpu.SemaphoreType.DMA((5,))],
        name="cut",
    )(offsets, acts)


def guarded(pair, mirrored, work):
    if pair in ONLY:
        pl.when(mirrored == ONLY[pair])(work)
    else:
        work()


def grams_kernel(flags, xs, xc, ys, yc, zs, zc, out, held, result, in_sems, out_sems):
    mirrored = flags[0]
    loads = [
        pltpu.make_async_copy(source, held.at[at], in_sems.at[at])
        for at, source in enumerate((xs, xc, ys, yc, zs, zc))
    ]
    for load in loads:
        load.start()
    for load in loads:
        load.wait()
    for pair, (one, two, _) in enumerate(PAIRS):
        slot = SLOT[pair]

        def work(one=one, two=two, slot=slot):
            result[slot] = lax.dot_general(
                held[one], held[two], NT, preferred_element_type=jnp.float32
            )
            pltpu.make_async_copy(result.at[slot], out.at[slot], out_sems.at[slot]).start()

        guarded(pair, mirrored, work)
    for slot in range(7):
        pltpu.make_async_copy(result.at[slot], out.at[slot], out_sems.at[slot]).wait()


def grams(flags, blocks):
    rows, width = blocks[0].shape
    return pl.pallas_call(
        grams_kernel,
        in_specs=[pl.BlockSpec(memory_space=pltpu.SMEM)] + [pl.BlockSpec(memory_space=pl.ANY)] * 6,
        out_specs=pl.BlockSpec(memory_space=pl.ANY),
        out_shape=jax.ShapeDtypeStruct((7, rows, rows), jnp.float32),
        scratch_shapes=[
            pltpu.VMEM((6, rows, width), blocks[0].dtype),
            pltpu.VMEM((7, rows, rows), jnp.float32),
            pltpu.SemaphoreType.DMA((6,)),
            pltpu.SemaphoreType.DMA((7,)),
        ],
        compiler_params=pltpu.CompilerParams(vmem_limit_bytes=VMEM_BYTES),
        cost_estimate=pl.CostEstimate(
            flops=14 * rows * rows * width,
            bytes_accessed=12 * rows * width + 28 * rows * rows,
            transcendentals=0,
        ),
        name="grams",
    )(flags, *blocks)


def token_sums(one, two, gram, sums):
    rows = one.shape[0]
    step = math.gcd(rows, 256)
    for at in range(0, rows, step):
        cols = slice(at, at + step)
        inner = lax.dot_general(one[...], two[cols, :], NT, preferred_element_type=jnp.float32)
        weighted = inner * gram[:, cols]
        sums[:, cols] = weighted.reshape(rows // TOK, TOK, step).sum(axis=1)


def three_parts(value):
    high = value.astype(jnp.bfloat16)
    rest = value - high.astype(jnp.float32)
    middle = rest.astype(jnp.bfloat16)
    low = (rest - middle.astype(jnp.float32)).astype(jnp.bfloat16)
    return high, middle, low


def dot_parts(value, table):
    total = None
    for part in reversed(three_parts(value)):
        term = jnp.dot(part, table, preferred_element_type=jnp.float32)
        total = term if total is None else total + term
    return total


def tiles_of(sums, gather):
    count, examples, rows = sums.shape
    flat = dot_parts(sums[...].reshape(count * examples, rows), gather[...])
    return flat.reshape(count, examples, LANES)


def first_kernel(flags, gather, acts, x_half, ys, zs, gram, out,
                 xs_v, xc_v, ys_v, zs_v, own_v, half_v, gram_v, sums, sems):
    mirrored, work_at, half_at, in_half = flags[0], flags[1], flags[2], flags[3]
    quarter = ys.shape[1]
    loads = {
        "xs": (acts.at[:, pl.ds(pl.multiple_of(work_at, LANES), quarter)], xs_v),
        "ys": (ys, ys_v),
        "g0": (gram.at[0], gram_v.at[0]),
        "zs": (zs, zs_v),
        "g1": (gram.at[1], gram_v.at[1]),
        "xc": (x_half.at[:, pl.ds(pl.multiple_of(in_half, LANES), quarter)], xc_v),
        "g2": (gram.at[2], gram_v.at[2]),
        "own": (acts.at[:, pl.ds(pl.multiple_of(half_at, LANES), 2 * quarter)], own_v),
        "half": (x_half, half_v),
        "g3": (gram.at[3], gram_v.at[3]),
    }
    copies = {
        key: pltpu.make_async_copy(source, target, sems.at[at])
        for at, (key, (source, target)) in enumerate(loads.items())
    }
    for copy in copies.values():
        copy.start()
    plan = (
        (("xs", "ys", "g0"), xs_v, ys_v),
        (("zs", "g1"), ys_v, zs_v),
        (("xc", "g2"), xc_v, ys_v),
        (("own", "half", "g3"), own_v, half_v),
    )
    for at, pair in enumerate(FIRST):
        keys, one, two = plan[at]
        for key in keys:
            copies[key].wait()
        if pair in ONLY:
            sums[at] = jnp.zeros(sums.shape[1:], jnp.float32)
        guarded(pair, mirrored, functools.partial(token_sums, one, two, gram_v.at[at], sums.at[at]))
    out[...] = tiles_of(sums, gather)


def second_kernel(flags, weights, gather, hot, first_tiles, acts, x_half, ys, yc, zs, zc, gram,
                  out, xs_v, xc_v, ys_v, yc_v, zs_v, zc_v, gram_v, sums, table, sems):
    mirrored, work_at, in_half = flags[0], flags[1], flags[3]
    quarter = ys.shape[1]
    loads = {
        "yc": (yc, yc_v),
        "xc": (x_half.at[:, pl.ds(pl.multiple_of(in_half, LANES), quarter)], xc_v),
        "g4": (gram.at[4], gram_v.at[0]),
        "zc": (zc, zc_v),
        "g5": (gram.at[5], gram_v.at[1]),
        "ys": (ys, ys_v),
        "zs": (zs, zs_v),
        "g6": (gram.at[6], gram_v.at[2]),
        "xs": (acts.at[:, pl.ds(pl.multiple_of(work_at, LANES), quarter)], xs_v),
        "g2": (gram.at[2], gram_v.at[3]),
    }
    copies = {
        key: pltpu.make_async_copy(source, target, sems.at[at])
        for at, (key, (source, target)) in enumerate(loads.items())
    }
    for copy in copies.values():
        copy.start()
    plan = (
        (("yc", "xc", "g4"), xc_v, yc_v, 0),
        (("zc", "g5"), yc_v, zc_v, 1),
        (("ys", "zs", "g6"), yc_v, zs_v, 2),
        ((), ys_v, zc_v, 2),
        (("xs", "g2"), xs_v, yc_v, 3),
    )
    table[...] = jnp.zeros_like(table)
    for at, pair in enumerate(SECOND):
        keys, one, two, slot = plan[at]
        for key in keys:
            copies[key].wait()
        if pair in ONLY:
            sums[at] = jnp.zeros(sums.shape[1:], jnp.float32)
        guarded(pair, mirrored, functools.partial(token_sums, one, two, gram_v.at[slot], sums.at[at]))
    later = tiles_of(sums, gather)
    examples = sums.shape[1]
    for pair, (one, two, _) in enumerate(PAIRS):
        tile = first_tiles[pair] if pair < len(FIRST) else later[pair - len(FIRST)]
        tile = tile * weights[pair]
        table[one * LANES:one * LANES + examples, two * LANES:(two + 1) * LANES] = tile
        full = jnp.concatenate([tile, jnp.zeros((LANES - examples, LANES), jnp.float32)], axis=0)
        table[two * LANES:(two + 1) * LANES, one * LANES:(one + 1) * LANES] = full.T
    total = dot_parts(table[...], hot[...])
    for block in range(6):
        out[block] = total[block * LANES:block * LANES + examples, :DOMAINS]


def per_device(acts, grads, domain, listed):
    rows, width = acts.shape
    examples = rows // TOK
    quarter = width // 4
    count = lax.axis_size("ex")
    me = lax.axis_index("ex")
    core = me % 2
    side = (me // 2) % 2
    mirrored = core ^ side
    bf16 = acts.dtype

    def work_at(side_at, core_at):
        return core_at * 2 * quarter + (1 - side_at) * quarter

    flags = jnp.stack([
        mirrored, work_at(side, core), core * 2 * quarter, (1 - side) * quarter
    ]).astype(jnp.int32)
    offsets = jnp.stack([
        work_at(1 - side, core),
        work_at(side, core),
        (1 - core) * 2 * quarter,
        work_at(1 - side, 1 - core),
        work_at(side, 1 - core),
    ]).astype(jnp.int32)

    grads_ys = send(grads, across, 0)
    grads_zs = send(grads, along, 0)
    grads_xc = send(grads, stay, 1)
    cut_ys, cut_zs, cut_xh, cut_yc, cut_zc = cut(acts, offsets)
    ys = send(cut_ys, across, 0)
    zs = send(cut_zs, along, 0)
    x_half = send(cut_xh, stay, 1)
    yc = send(cut_yc, across, 1)
    zc = send(cut_zc, along, 1)
    grads_yc = send(grads_ys, stay, 1)
    grads_zc = send(grads_zs, stay, 1)

    info = jnp.concatenate([domain, listed[0], jnp.zeros((LANES - examples - 2,), jnp.int32)])
    every = lax.all_gather(info, "ex")
    zs_at = jnp.where(side == 0, me + 4, me + count - 4) % count
    ids = jnp.stack([me, me ^ 1, me ^ 2, me ^ 3, zs_at, zs_at ^ 1])
    near = every[ids]
    domains = jnp.where(jnp.arange(LANES)[None, :] < examples, near, -1)
    hot = (domains.reshape(6 * LANES)[:, None] == jnp.arange(LANES)[None, :]).astype(jnp.bfloat16)
    flag = near[:, examples:examples + 2].astype(jnp.float32)
    factor = 1.0 / (TOK * math.sqrt(width * grads.shape[1]))
    weights = []
    for one, two, apart in PAIRS:
        if (one, two) == (XS, XC):
            chosen = jnp.where(core == 0, flag[XS, apart], flag[XC, apart])
        else:
            chosen = jnp.where(side == 0, flag[one, apart], flag[two, apart])
        weights.append(chosen * factor)
    weights = jnp.stack(weights)

    gram = grams(flags, (grads, grads_xc, grads_ys, grads_yc, grads_zs, grads_zc))
    gather = (
        (jnp.arange(rows) // TOK)[:, None] == jnp.arange(LANES)[None, :]
    ).astype(jnp.bfloat16)

    smem = pl.BlockSpec(memory_space=pltpu.SMEM)
    vmem = pl.BlockSpec(memory_space=pltpu.VMEM)
    hbm = pl.BlockSpec(memory_space=pl.ANY)
    params = pltpu.CompilerParams(vmem_limit_bytes=VMEM_BYTES)
    slice_v = pltpu.VMEM((rows, quarter), bf16)
    half_v = pltpu.VMEM((rows, 2 * quarter), bf16)
    gram_v = pltpu.VMEM((4, rows, rows), jnp.float32)
    first_tiles = pl.pallas_call(
        first_kernel,
        in_specs=[smem, vmem] + [hbm] * 5,
        out_specs=vmem,
        out_shape=jax.ShapeDtypeStruct((4, examples, LANES), jnp.float32),
        scratch_shapes=[slice_v] * 4 + [half_v] * 2 + [
            gram_v,
            pltpu.VMEM((4, examples, rows), jnp.float32),
            pltpu.SemaphoreType.DMA((10,)),
        ],
        compiler_params=params,
        cost_estimate=pl.CostEstimate(
            flops=10 * rows * rows * quarter,
            bytes_accessed=20 * rows * quarter + 16 * rows * rows,
            transcendentals=0,
        ),
        name="first",
    )(flags, gather, acts, x_half, ys, zs, gram)
    sums = pl.pallas_call(
        second_kernel,
        in_specs=[smem, smem, vmem, vmem, vmem] + [hbm] * 7,
        out_specs=vmem,
        out_shape=jax.ShapeDtypeStruct((6, examples, DOMAINS), jnp.float32),
        scratch_shapes=[slice_v] * 6 + [
            gram_v,
            pltpu.VMEM((5, examples, rows), jnp.float32),
            pltpu.VMEM((6 * LANES, 6 * LANES), jnp.float32),
            pltpu.SemaphoreType.DMA((10,)),
        ],
        compiler_params=params,
        cost_estimate=pl.CostEstimate(
            flops=8 * rows * rows * quarter,
            bytes_accessed=12 * rows * quarter + 16 * rows * rows,
            transcendentals=0,
        ),
        name="second",
    )(flags, weights, gather, hot, first_tiles, acts, x_half, ys, yc, zs, zc, gram)

    total = sums[XS]
    total = total + send(sums[XC], stay, 1)
    total = total + send(sums[YS], across, 0)
    total = total + send(sums[YC], across, 1)
    total = total + send(sums[ZS], against, 0)
    total = total + send(sums[ZC], against, 1)
    return total


def solution(mesh):
    in_specs = (
        P(("groups", "ex"), None),
        P(("groups", "ex"), None),
        P(("groups", "ex")),
        P(("groups", "ex"), None),
    )
    out_specs = P(("groups", "ex"), None)
    return jax.shard_map(
        per_device, mesh=mesh, in_specs=in_specs, out_specs=out_specs, check_vma=False
    )
```

time: 334 us -> 511 us (1.53)
  Pallas kernels: 0 us -> 405 us
  waiting for transfers between devices: 210 us -> 15.5 us
  blocking collectives: 0 us -> 58 us
  local copies, waits for them, and re-layouts: 47.6 us -> 5.5 us
  matrix products: 27.8 us -> 0 us
  other arithmetic: 27.6 us -> 2.63 us
  between operations: 1.4 us -> 11.3 us
  starting transfers between devices: 19.4 us -> 13.6 us
    pallas_call x0 -> x4, Pallas kernels: none -> 405 us  [the longest x1 359 us: cut(): pl.pallas_call(cut_kernel, in_specs=[pl.BlockSpec(memory_space=pltpu.SMEM...]
    ppermute x8 -> x15, waiting for transfers between devices: 210 us -> 15.5 us  [send(): return lax.ppermute(value, 'ex', pairs)]
    all_gather x0 -> x1, blocking collectives: none -> 58 us  [per_device(): every = lax.all_gather(info, 'ex')]
    reshape x2 -> x0, local copies, waits for them, and re-layouts: 46.2 us -> none  [pair_scores(): (inner_acts * inner_grads).reshape(per_block, TOK, per_block, TOK)]
    dot_general x8 -> x0, matrix products: 27.8 us -> none  [the longest x2 20.2 us: pair_scores(): lax.dot_general(acts_one, acts_two, contract, preferred_element_type=jnp....]
    reduce_sum x2 -> x0, other arithmetic: 27.6 us -> none  [pair_scores(): (inner_acts * inner_grads).reshape(per_block, TOK, per_block, TOK)]
    ppermute x8 -> x15, starting transfers between devices: 19.4 us -> 13.6 us  [send(): return lax.ppermute(value, 'ex', pairs)]
  transfers between devices with their start and end apart: 8 -> 15, of which waited for: 4 -> 4; matrix products, arithmetic and copies ran while one was open for 31% -> 1% of each run, Pallas kernels for 0% -> 76%
where the time goes in v1:
time: 511 us
  Pallas kernels  405 us (79%)
  blocking collectives  58 us (11%)
  waiting for transfers between devices  15.5 us (3%)
  starting transfers between devices  13.6 us (3%)
  between operations  11.3 us (2%)
  local copies, waits for them, and re-layouts  5.5 us (1%)
    pallas_call x1, Pallas kernels, cut(): pl.pallas_call(cut_kernel, in_specs=[pl.BlockSpec(memory_space=pltpu.SMEM...  359 us
    all_gather x1, blocking collectives, per_device(): every = lax.all_gather(info, 'ex')  58 us
    pallas_call x1, Pallas kernels, per_device(): pl.pallas_call(first_kernel, in_specs=[smem, vmem] + [hbm] * 5, out_specs...  15.5 us
    ppermute x15, waiting for transfers between devices, send(): return lax.ppermute(value, 'ex', pairs)  15.5 us
    pallas_call x1, Pallas kernels, grams(): pl.pallas_call(grams_kernel, in_specs=[pl.BlockSpec(memory_space=pltpu.SM...  15.4 us
    pallas_call x1, Pallas kernels, per_device(): pl.pallas_call(second_kernel, in_specs=[smem, smem, vmem, vmem, vmem] + [...  14.4 us
    ppermute x15, starting transfers between devices, send(): return lax.ppermute(value, 'ex', pairs)  13.6 us
  transfers between devices with their start and end apart: 15, of which 4 were waited for; matrix products, arithmetic and copies ran while one was open for 1% of the time, Pallas kernels for 76%

profile of v1, /device:TPU:0, one launch (start us, length us, event | category | flops | bytes accessed | tf_op | source)
XLA Modules:
  0.0 511.0 jit_solution(8576651907323309408)
XLA Ops:
  0.0 3.0 collective-permute-start.4
  3.0 3.6 collective-permute-start.6
  6.6 0.7 stack.108.offsets
  7.3 359.3 %cut.1 = (bf16[768,1280]{1,0:T(8,128)(2,1)}, bf16[768,1280]{1,0:T(8,128)(2,1)}, bf16[768,2560]{1,0:T(8,128)(2,1)}, bf16[768,1280]{1,0:T(8,128)(2,1)}, bf16[768,1280]{1,0:T(8,128)(2,1)}) custom-call(s32[5]{0:T(128)} %stack.108.offsets, bf16[768,5120]{1,0:T(8,128)(2,1)} %acts.5), custom_call_target="tpu_custom_call" | custom-call | tf_op jit(solution)/shard_map/cut/pallas_call | solution.py:69
  366.6 0.5 collective-permute-start.3
  367.8 9.3 %collective-permute-done.3.xc = bf16[768,1024]{1,0:T(8,128)(2,1)} collective-permute-done((bf16[768,1024]{1,0:T(8,128)(2,1)S(1)}, bf16[768,1024]{1,0:T(8,128)(2,1)}, u32[]{:S(2)}, u32[]{:S(2)}) %collective-permute-start.3) | collective-permute-done | bytes 1572896 | tf_op jit(solution)/shard_map/ppermute | solution.py:51
  377.7 58.0 %all-gather.1 = s32[16,1,128]{2,1,0:T(1,128)S(1)} all-gather(s32[1,1,128]{2,1,0:T(1,128)S(1)} %add_bitcast_fusion), channel_id=2, replica_groups=mesh['groups'=2,'ex'=16] {'ex'}, dimensions={0}, use_global_device_ids=true | all-gather | bytes 8704 | tf_op jit(solution)/shard_map/all_gather | solution.py:291
  435.6 0.6 gather_fusion
  436.3 0.7 fusion.11
  437.1 0.6 pad_add_fusion.flags
  448.9 0.6 stack.103.weights
  449.5 1.0 fusion
  450.6 15.4 %grams.1.gram = f32[7,768,768]{2,1,0:T(8,128)} custom-call(s32[4]{0:T(128)} %pad_add_fusion.flags, bf16[768,1024]{1,0:T(8,128)(2,1)} %xs.1, bf16[768,1024]{1,0:T(8,128)(2,1)} %collective-permute-done.3.xc, bf16[768,1024]{1,0:T(8,128)(2,1)} %collective-permute-done.4.ys, bf16[768,1024]{1,0:T(8,128)(2,1)} %collective-permute-done.5.yc, ...), custom_call_target="tpu_custom_call" | custom-call | flops 8455716864 | bytes 25952256 | tf_op jit(solution)/shard_map/grams/pallas_call | solution.py:112
  466.0 1.2 copy-done
  467.2 15.5 %first.1.first_tiles = f32[4,96,128]{2,1,0:T(8,128)} custom-call(s32[4]{0:T(128)} %pad_add_fusion.flags, bf16[768,128]{1,0:T(8,128)(2,1)} %get-tuple-element.32.gather, bf16[768,5120]{1,0:T(8,128)(2,1)} %acts.5, bf16[768,2560]{1,0:T(8,128)(2,1)} %collective-permute-done.x_half, bf16[768,1280]{1,0:T(8,128)(2,1)} %copy-done, ...), custom_call_target="tpu_custom_call" | custom-call | flops 7549747200 | bytes 29097984 | tf_op jit(solution)/shard_map/first/pallas_call | solution.py:320
  482.7 14.4 %second.1 = f32[6,96,48]{2,1,0:T(8,128)} custom-call(s32[4]{0:T(128)} %pad_add_fusion.flags, f32[9]{0:T(128)} %stack.103.weights, bf16[768,128]{1,0:T(8,128)(2,1)} %get-tuple-element.32.gather, bf16[768,128]{1,0:T(8,128)(2,1)} %get-tuple-element.33.hot, f32[4,96,128]{2,1,0:T(8,128)} %first.1.first_tiles, bf16[768,5120]{1,0:T(8,128)(2,1)} %acts.5, ...), custom_call_target="tpu_custom_call" | custom-call | flops 6039797760 | bytes 21233664 | tf_op jit(solution)/shard_map/second/pallas_call | solution.py:338
  497.1 0.9 slice_bitcast_fusion.4
  498.1 1.6 collective-permute-start.10
  499.7 3.6 collective-permute-start.11
  503.4 2.3 collective-permute-done.11
  505.6 1.4 collective-permute-done.12
  507.0 2.5 collective-permute-done.13
  509.5 0.8 fusion.6
  510.3 0.7 copy.7
  (37 shorter events, 1.6 us)
Async XLA Ops:
  0.0 367.1 %collective-permute-start.4 = (bf16[768,1024]{1,0:T(8,128)(2,1)}, bf16[768,1024]{1,0:T(8,128)(2,1)}, u32[]{:S(2)}, u32[]{:S(2)}) collective-permute-start(bf16[768,1024]{1,0:T(8,128)(2,1)} %xs.1), channel_id=1, source_target_pairs={{0,2},{1,3},{2,0},{3,1},{4,6},{5,7},{6,4},{7,5},{8,10},{9,11},{10,... | collective-permute-start | bytes 4718600 | tf_op jit(solution)/shard_map/ppermute | solution.py:51
  3.0 364.3 %collective-permute-start.6 = (bf16[768,1024]{1,0:T(8,128)(2,1)}, bf16[768,1024]{1,0:T(8,128)(2,1)}, u32[]{:S(2)}, u32[]{:S(2)}) collective-permute-start(bf16[768,1024]{1,0:T(8,128)(2,1)} %xs.1), channel_id=1, source_target_pairs={{0,12},{1,13},{2,6},{3,7},{4,0},{5,1},{6,10},{7,11},{8,4},{9,5},{1... | collective-permute-start | bytes 4718600 | tf_op jit(solution)/shard_map/ppermute | solution.py:51
  7.2 359.4 %copy-start.3 = (bf16[768,1024]{1,0:T(8,128)(2,1)S(1)}, bf16[768,1024]{1,0:T(8,128)(2,1)}, u32[]{:S(2)}) copy-start(bf16[768,1024]{1,0:T(8,128)(2,1)} %xs.1) | copy-start | bytes 4718596
  7.2 370.3 %copy-start.1 = (s32[1,2]{1,0:T(1,128)S(1)}, s32[1,2]{1,0:T(1,128)}, u32[]{:S(2)}) copy-start(s32[1,2]{1,0:T(1,128)} %param.7) | copy-start | bytes 28
  7.3 370.3 %copy-start.2 = (s32[96]{0:T(128)S(1)}, s32[96]{0:T(128)}, u32[]{:S(2)}) copy-start(s32[96]{0:T(128)} %param.6) | copy-start | bytes 1156
  366.6 99.4 %collective-permute-start = (bf16[768,2560]{1,0:T(8,128)(2,1)}, bf16[768,2560]{1,0:T(8,128)(2,1)}, u32[]{:S(2)}, u32[]{:S(2)}) collective-permute-start(bf16[768,2560]{1,0:T(8,128)(2,1)} %get-tuple-element.10), channel_id=1, source_target_pairs={{0,1},{1,0},{2,3},{3,2},{4,5},{5,4},{6,7},{7,6},{8,9},{9,8},{10,11... | collective-permute-start | bytes 11796488 | tf_op jit(solution)/shard_map/ppermute | solution.py:51
  366.6 10.5 %collective-permute-start.3 = (bf16[768,1024]{1,0:T(8,128)(2,1)S(1)}, bf16[768,1024]{1,0:T(8,128)(2,1)}, u32[]{:S(2)}, u32[]{:S(2)}) collective-permute-start(bf16[768,1024]{1,0:T(8,128)(2,1)S(1)} %copy-done.3), channel_id=1, source_target_pairs={{0,1},{1,0},{2,3},{3,2},{4,5},{5,4},{6,7},{7,6},{8,9},{9,8},{10,11... | collective-permute-start | bytes 4718600 | tf_op jit(solution)/shard_map/ppermute | solution.py:51
  367.1 69.8 %collective-permute-start.5 = (bf16[768,1024]{1,0:T(8,128)(2,1)}, bf16[768,1024]{1,0:T(8,128)(2,1)}, u32[]{:S(2)}, u32[]{:S(2)}) collective-permute-start(bf16[768,1024]{1,0:T(8,128)(2,1)} %collective-permute-done.4.ys), channel_id=1, source_target_pairs={{0,1},{1,0},{2,3},{3,2},{4,5},{5,4},{6,7},{7,6},{8,9},{9,8},{10,11... | collective-permute-start | bytes 4718600 | tf_op jit(solution)/shard_map/ppermute | solution.py:51
  367.2 69.8 %collective-permute-start.7 = (bf16[768,1024]{1,0:T(8,128)(2,1)}, bf16[768,1024]{1,0:T(8,128)(2,1)}, u32[]{:S(2)}, u32[]{:S(2)}) collective-permute-start(bf16[768,1024]{1,0:T(8,128)(2,1)} %collective-permute-done.6.zs), channel_id=1, source_target_pairs={{0,1},{1,0},{2,3},{3,2},{4,5},{5,4},{6,7},{7,6},{8,9},{9,8},{10,11... | collective-permute-start | bytes 4718600 | tf_op jit(solution)/shard_map/ppermute | solution.py:51
  367.6 98.3 %collective-permute-start.1 = (bf16[768,1280]{1,0:T(8,128)(2,1)}, bf16[768,1280]{1,0:T(8,128)(2,1)S(1)}, u32[]{:S(2)}, u32[]{:S(2)}) collective-permute-start(bf16[768,1280]{1,0:T(8,128)(2,1)} %get-tuple-element.11), channel_id=1, source_target_pairs={{0,2},{1,3},{2,0},{3,1},{4,6},{5,7},{6,4},{7,5},{8,10},{9,11},{10,... | collective-permute-start | bytes 5898248 | tf_op jit(solution)/shard_map/ppermute | solution.py:51
  377.1 88.9 %collective-permute-start.2 = (bf16[768,1280]{1,0:T(8,128)(2,1)}, bf16[768,1280]{1,0:T(8,128)(2,1)}, u32[]{:S(2)}, u32[]{:S(2)}) collective-permute-start(bf16[768,1280]{1,0:T(8,128)(2,1)} %get-tuple-element.12), channel_id=1, source_target_pairs={{0,12},{1,13},{2,6},{3,7},{4,0},{5,1},{6,10},{7,11},{8,4},{9,5},{1... | collective-permute-start | bytes 5898248 | tf_op jit(solution)/shard_map/ppermute | solution.py:51
  437.0 45.7 %collective-permute-start.8 = (bf16[768,1280]{1,0:T(8,128)(2,1)}, bf16[768,1280]{1,0:T(8,128)(2,1)}, u32[]{:S(2)}, u32[]{:S(2)}) collective-permute-start(bf16[768,1280]{1,0:T(8,128)(2,1)} %get-tuple-element.13), channel_id=1, source_target_pairs={{0,3},{1,2},{2,1},{3,0},{4,7},{5,6},{6,5},{7,4},{8,11},{9,10},{10,... | collective-permute-start | bytes 5898248 | tf_op jit(solution)/shard_map/ppermute | solution.py:51
  437.1 45.6 %collective-permute-start.9 = (bf16[768,1280]{1,0:T(8,128)(2,1)}, bf16[768,1280]{1,0:T(8,128)(2,1)}, u32[]{:S(2)}, u32[]{:S(2)}) collective-permute-start(bf16[768,1280]{1,0:T(8,128)(2,1)} %get-tuple-element.14), channel_id=1, source_target_pairs={{0,13},{1,12},{2,7},{3,6},{4,1},{5,0},{6,11},{7,10},{8,5},{9,4},{1... | collective-permute-start | bytes 5898248 | tf_op jit(solution)/shard_map/ppermute | solution.py:51
  465.9 1.3 copy-start
  498.1 5.3 %collective-permute-start.10 = (f32[96,48]{1,0:T(8,128)S(1)}, f32[96,48]{1,0:T(8,128)S(1)}, u32[]{:S(2)}, u32[]{:S(2)}) collective-permute-start(f32[96,48]{1,0:T(8,128)S(1)} %get-tuple-element.15), channel_id=1, source_target_pairs={{0,1},{1,0},{2,3},{3,2},{4,5},{5,4},{6,7},{7,6},{8,9},{9,8},{10,11... | collective-permute-start | bytes 55304 | tf_op jit(solution)/shard_map/ppermute | solution.py:51
  499.7 5.9 %collective-permute-start.11 = (f32[96,48]{1,0:T(8,128)S(1)}, f32[96,48]{1,0:T(8,128)S(1)}, u32[]{:S(2)}, u32[]{:S(2)}) collective-permute-start(f32[96,48]{1,0:T(8,128)S(1)} %get-tuple-element.19), channel_id=1, source_target_pairs={{0,2},{1,3},{2,0},{3,1},{4,6},{5,7},{6,4},{7,5},{8,10},{9,11},{10,... | collective-permute-start | bytes 55304 | tf_op jit(solution)/shard_map/ppermute | solution.py:51
  503.3 3.7 collective-permute-start.12
  503.4 6.1 %collective-permute-start.13 = (f32[96,48]{1,0:T(8,128)S(1)}, f32[96,48]{1,0:T(8,128)S(1)}, u32[]{:S(2)}, u32[]{:S(2)}) collective-permute-start(f32[96,48]{1,0:T(8,128)S(1)} %get-tuple-element.17), channel_id=1, source_target_pairs={{0,4},{1,5},{2,14},{3,15},{4,8},{5,9},{6,2},{7,3},{8,12},{9,13},{1... | collective-permute-start | bytes 55304 | tf_op jit(solution)/shard_map/ppermute | solution.py:51
  503.4 6.1 %collective-permute-start.14 = (f32[96,48]{1,0:T(8,128)S(1)}, f32[96,48]{1,0:T(8,128)S(1)}, u32[]{:S(2)}, u32[]{:S(2)}) collective-permute-start(f32[96,48]{1,0:T(8,128)S(1)} %get-tuple-element.16), channel_id=1, source_target_pairs={{0,5},{1,4},{2,15},{3,14},{4,9},{5,8},{6,3},{7,2},{8,13},{9,12},{1... | collective-permute-start | bytes 55304 | tf_op jit(solution)/shard_map/ppermute | solution.py:51

commit v2 on v1

v2 whole, which is shorter than its diff:
```python
import functools
import math

import jax
import jax.numpy as jnp
from jax import lax
from jax.experimental import pallas as pl
from jax.experimental.pallas import tpu as pltpu
from jax.sharding import PartitionSpec as P

TOK = 8
DOMAINS = 48
LANES = 128
VMEM_BYTES = 40 * 1024 * 1024

XS, XC, YS, YC, ZS, ZC = range(6)
PAIRS = (
    (XS, YS, 1), (YS, ZS, 1), (XC, YS, 0), (XS, XC, 0),
    (XC, YC, 1), (YC, ZC, 1), (YC, ZS, 0), (YS, ZC, 0), (XS, YC, 0),
)
ONLY = {2: 0, 6: 0, 7: 1, 8: 1}
SLOT = (0, 1, 2, 3, 4, 5, 6, 6, 2)
FIRST = (0, 1, 2, 3)
SECOND = (4, 5, 6, 7, 8)
NT = (((1,), (1,)), ((), ()))


def across(chip):
    return chip ^ 1


def along(chip):
    return chip + 2 if chip & 1 else chip - 2


def against(chip):
    return chip - 2 if chip & 1 else chip + 2


def stay(chip):
    return chip


def send(value, move, flip):
    chips = lax.axis_size("ex") // 2
    pairs = [
        (2 * chip + core, 2 * (move(chip) % chips) + (core ^ flip))
        for chip in range(chips)
        for core in range(2)
    ]
    return lax.ppermute(value, "ex", pairs)


def cut_kernel(places, *refs):
    for source, target in zip(refs[:5], refs[5:]):
        target[...] = source[...]


def cut(acts, places):
    rows, width = acts.shape
    quarter = width // 4
    widths = (quarter, quarter, 2 * quarter, quarter, quarter)
    step = math.gcd(rows, 96)
    return pl.pallas_call(
        cut_kernel,
        grid_spec=pltpu.PrefetchScalarGridSpec(
            num_scalar_prefetch=1,
            grid=(rows // step,),
            in_specs=[
                pl.BlockSpec((step, w), functools.partial(lambda at, i, p: (i, p[at]), at))
                for at, w in enumerate(widths)
            ],
            out_specs=[pl.BlockSpec((step, w), lambda i, p: (i, 0)) for w in widths],
        ),
        out_shape=[jax.ShapeDtypeStruct((rows, w), acts.dtype) for w in widths],
        compiler_params=pltpu.CompilerParams(vmem_limit_bytes=VMEM_BYTES),
        name="cut",
    )(places, acts, acts, acts, acts, acts)


def guarded(pair, mirrored, work):
    if pair in ONLY:
        pl.when(mirrored == ONLY[pair])(work)
    else:
        work()


def grams_kernel(flags, xs, xc, ys, yc, zs, zc, out, held, result, in_sems, out_sems):
    mirrored = flags[0]
    loads = [
        pltpu.make_async_copy(source, held.at[at], in_sems.at[at])
        for at, source in enumerate((xs, xc, ys, yc, zs, zc))
    ]
    for load in loads:
        load.start()
    for load in loads:
        load.wait()
    for pair, (one, two, _) in enumerate(PAIRS):
        slot = SLOT[pair]

        def work(one=one, two=two, slot=slot):
            result[slot] = lax.dot_general(
                held[one], held[two], NT, preferred_element_type=jnp.float32
            )
            pltpu.make_async_copy(result.at[slot], out.at[slot], out_sems.at[slot]).start()

        guarded(pair, mirrored, work)
    for slot in range(7):
        pltpu.make_async_copy(result.at[slot], out.at[slot], out_sems.at[slot]).wait()


def grams(flags, blocks):
    rows, width = blocks[0].shape
    return pl.pallas_call(
        grams_kernel,
        in_specs=[pl.BlockSpec(memory_space=pltpu.SMEM)] + [pl.BlockSpec(memory_space=pl.ANY)] * 6,
        out_specs=pl.BlockSpec(memory_space=pl.ANY),
        out_shape=jax.ShapeDtypeStruct((7, rows, rows), jnp.float32),
        scratch_shapes=[
            pltpu.VMEM((6, rows, width), blocks[0].dtype),
            pltpu.VMEM((7, rows, rows), jnp.float32),
            pltpu.SemaphoreType.DMA((6,)),
            pltpu.SemaphoreType.DMA((7,)),
        ],
        compiler_params=pltpu.CompilerParams(vmem_limit_bytes=VMEM_BYTES),
        cost_estimate=pl.CostEstimate(
            flops=14 * rows * rows * width,
            bytes_accessed=12 * rows * width + 28 * rows * rows,
            transcendentals=0,
        ),
        name="grams",
    )(flags, *blocks)


def token_sums(one, two, gram, sums):
    rows = one.shape[0]
    step = math.gcd(rows, 256)
    for at in range(0, rows, step):
        cols = slice(at, at + step)
        inner = lax.dot_general(one[...], two[cols, :], NT, preferred_element_type=jnp.float32)
        weighted = inner * gram[:, cols]
        sums[:, cols] = weighted.reshape(rows // TOK, TOK, step).sum(axis=1)


def two_parts(value):
    high = value.astype(jnp.bfloat16)
    return high, (value - high.astype(jnp.float32)).astype(jnp.bfloat16)


def dot_parts(value, table):
    high, low = two_parts(value)
    return lax.dot_general(low, table, NT, preferred_element_type=jnp.float32) + lax.dot_general(
        high, table, NT, preferred_element_type=jnp.float32
    )


def domain_sums(pairs, factor, flags, info, info_v, sums, table):
    count, examples, rows = sums.shape
    example = lax.broadcasted_iota(jnp.int32, (LANES, rows), 0)
    gather = (lax.broadcasted_iota(jnp.int32, (LANES, rows), 1) // TOK == example)
    tiles = dot_parts(sums[...].reshape(count * examples, rows), gather.astype(jnp.bfloat16))
    tiles = tiles.reshape(count, examples, LANES)
    core, side = flags[4], flags[5]
    table[...] = jnp.zeros_like(table)
    pad = jnp.zeros((LANES - examples, LANES), jnp.float32)
    for at, pair in enumerate(pairs):
        one, two, apart = PAIRS[pair]
        here, there = info[one, examples + apart], info[two, examples + apart]
        own = (one, two) == (XS, XC)
        flag = jnp.where((core if own else side) == 0, here, there)
        tile = jnp.concatenate([tiles[at], pad], axis=0) * (flag.astype(jnp.float32) * factor)
        table[one * LANES:(one + 1) * LANES, two * LANES:(two + 1) * LANES] = tile
        table[two * LANES:(two + 1) * LANES, one * LANES:(one + 1) * LANES] = tile.T
    row = lax.broadcasted_iota(jnp.int32, (LANES, LANES), 0)
    inside = lax.broadcasted_iota(jnp.int32, (LANES, LANES), 1) < examples
    hot = jnp.concatenate(
        [((info_v[block:block + 1, :] == row) & inside).astype(jnp.bfloat16) for block in range(6)],
        axis=1,
    )
    return dot_parts(table[...], hot)


def staged(loads, sems, plan):
    copies = {
        key: pltpu.make_async_copy(source, target, sems.at[at])
        for at, (key, (source, target)) in enumerate(loads.items())
    }

    def start(at):
        if at < len(plan):
            for key in plan[at][0]:
                copies[key].start()

    def ready(at):
        if at == 0:
            start(0)
        for key in plan[at][0]:
            copies[key].wait()
        start(at + 1)

    return ready


def first_kernel(factor, flags, info, info_v, acts, x_half, ys, zs, gram, out,
                 xs_v, xc_v, ys_v, zs_v, own_v, half_v, gram_v, sums, table, sems):
    mirrored, work_at, half_at, in_half = flags[0], flags[1], flags[2], flags[3]
    quarter = ys.shape[1]
    loads = {
        "xs": (acts.at[:, pl.ds(pl.multiple_of(work_at, LANES), quarter)], xs_v),
        "ys": (ys, ys_v),
        "g0": (gram.at[0], gram_v.at[0]),
        "zs": (zs, zs_v),
        "g1": (gram.at[1], gram_v.at[1]),
        "xc": (x_half.at[:, pl.ds(pl.multiple_of(in_half, LANES), quarter)], xc_v),
        "g2": (gram.at[2], gram_v.at[2]),
        "own": (acts.at[:, pl.ds(pl.multiple_of(half_at, LANES), 2 * quarter)], own_v),
        "half": (x_half, half_v),
        "g3": (gram.at[3], gram_v.at[3]),
    }
    plan = (
        (("xs", "ys", "g0"), xs_v, ys_v),
        (("zs", "g1"), ys_v, zs_v),
        (("xc", "g2"), xc_v, ys_v),
        (("own", "half", "g3"), own_v, half_v),
    )
    ready = staged(loads, sems, plan)
    for at, pair in enumerate(FIRST):
        _, one, two = plan[at]
        ready(at)
        if pair in ONLY:
            sums[at] = jnp.zeros(sums.shape[1:], jnp.float32)
        guarded(pair, mirrored, functools.partial(token_sums, one, two, gram_v.at[at], sums.at[at]))
    out[...] = domain_sums(FIRST, factor, flags, info, info_v, sums, table)


def second_kernel(factor, flags, info, info_v, earlier, acts, x_half, ys, yc, zs, zc, gram,
                  *rest):
    outs = rest[:6]
    xs_v, xc_v, ys_v, yc_v, zs_v, zc_v, gram_v, sums, table, sems = rest[6:]
    mirrored, work_at, in_half = flags[0], flags[1], flags[3]
    quarter = ys.shape[1]
    loads = {
        "yc": (yc, yc_v),
        "xc": (x_half.at[:, pl.ds(pl.multiple_of(in_half, LANES), quarter)], xc_v),
        "g4": (gram.at[4], gram_v.at[0]),
        "zc": (zc, zc_v),
        "g5": (gram.at[5], gram_v.at[1]),
        "ys": (ys, ys_v),
        "zs": (zs, zs_v),
        "g6": (gram.at[6], gram_v.at[2]),
        "xs": (acts.at[:, pl.ds(pl.multiple_of(work_at, LANES), quarter)], xs_v),
        "g2": (gram.at[2], gram_v.at[3]),
    }
    plan = (
        (("yc", "xc", "g4"), xc_v, yc_v, 0),
        (("zc", "g5"), yc_v, zc_v, 1),
        (("ys", "zs", "g6"), yc_v, zs_v, 2),
        (("xs", "g2"), ys_v, zc_v, 2),
        ((), xs_v, yc_v, 3),
    )
    ready = staged(loads, sems, plan)
    for at, pair in enumerate(SECOND):
        _, one, two, slot = plan[at]
        ready(at)
        if pair in ONLY:
            sums[at] = jnp.zeros(sums.shape[1:], jnp.float32)
        guarded(pair, mirrored, functools.partial(token_sums, one, two, gram_v.at[slot], sums.at[at]))
    total = (earlier[...] + domain_sums(SECOND, factor, flags, info, info_v, sums, table)).T
    examples = sums.shape[1]
    for block, out in enumerate(outs):
        out[...] = total[:DOMAINS, block * LANES:block * LANES + examples]


def per_device(acts, grads, domain, listed):
    rows, width = acts.shape
    examples = rows // TOK
    quarter = width // 4
    me = lax.axis_index("ex")
    core = me % 2
    side = (me // 2) % 2
    mirrored = core ^ side

    def work_at(side_at, core_at):
        return core_at * 2 * quarter + (1 - side_at) * quarter

    flags = jnp.stack([
        mirrored, work_at(side, core), core * 2 * quarter, (1 - side) * quarter, core, side
    ]).astype(jnp.int32)
    places = jnp.stack([
        core * 2 + side,
        core * 2 + (1 - side),
        1 - core,
        (1 - core) * 2 + side,
        (1 - core) * 2 + (1 - side),
    ]).astype(jnp.int32)

    grads_ys = send(grads, across, 0)
    grads_zs = send(grads, along, 0)
    cut_ys, cut_zs, cut_xh, cut_yc, cut_zc = cut(acts, places)
    ys = send(cut_ys, across, 0)
    zs = send(cut_zs, along, 0)
    grads_xc = send(grads, stay, 1)
    x_half = send(cut_xh, stay, 1)
    yc = send(cut_yc, across, 1)
    zc = send(cut_zc, along, 1)
    grads_yc = send(grads_ys, stay, 1)
    grads_zc = send(grads_zs, stay, 1)

    own_info = jnp.concatenate(
        [domain, listed[0], jnp.zeros((LANES - examples - 2,), jnp.int32)]
    )[None, :]
    info = jnp.concatenate([
        own_info,
        send(own_info, stay, 1),
        send(own_info, across, 0),
        send(own_info, across, 1),
        send(own_info, along, 0),
        send(own_info, along, 1),
    ])
    factor = 1.0 / (TOK * math.sqrt(width * grads.shape[1]))

    gram = grams(flags, (grads, grads_xc, grads_ys, grads_yc, grads_zs, grads_zc))

    smem = pl.BlockSpec(memory_space=pltpu.SMEM)
    vmem = pl.BlockSpec(memory_space=pltpu.VMEM)
    hbm = pl.BlockSpec(memory_space=pl.ANY)
    params = pltpu.CompilerParams(vmem_limit_bytes=VMEM_BYTES)
    slice_v = pltpu.VMEM((rows, quarter), acts.dtype)
    half_v = pltpu.VMEM((rows, 2 * quarter), acts.dtype)
    gram_v = pltpu.VMEM((4, rows, rows), jnp.float32)
    table_v = pltpu.VMEM((6 * LANES, 6 * LANES), jnp.float32)
    first = pl.pallas_call(
        functools.partial(first_kernel, factor),
        in_specs=[smem, smem, vmem] + [hbm] * 5,
        out_specs=vmem,
        out_shape=jax.ShapeDtypeStruct((6 * LANES, LANES), jnp.float32),
        scratch_shapes=[slice_v] * 4 + [half_v] * 2 + [
            gram_v,
            pltpu.VMEM((4, examples, rows), jnp.float32),
            table_v,
            pltpu.SemaphoreType.DMA((10,)),
        ],
        compiler_params=params,
        cost_estimate=pl.CostEstimate(
            flops=10 * rows * rows * quarter,
            bytes_accessed=20 * rows * quarter + 16 * rows * rows,
            transcendentals=0,
        ),
        name="first",
    )(flags, info, info, acts, x_half, ys, zs, gram)
    sums = pl.pallas_call(
        functools.partial(second_kernel, factor),
        in_specs=[smem, smem, vmem, vmem] + [hbm] * 7,
        out_specs=[vmem] * 6,
        out_shape=[jax.ShapeDtypeStruct((DOMAINS, examples), jnp.float32)] * 6,
        scratch_shapes=[slice_v] * 6 + [
            gram_v,
            pltpu.VMEM((5, examples, rows), jnp.float32),
            table_v,
            pltpu.SemaphoreType.DMA((10,)),
        ],
        compiler_params=params,
        cost_estimate=pl.CostEstimate(
            flops=8 * rows * rows * quarter,
            bytes_accessed=12 * rows * quarter + 16 * rows * rows,
            transcendentals=0,
        ),
        name="second",
    )(flags, info, info, first, acts, x_half, ys, yc, zs, zc, gram)

    total = sums[XS]
    total = total + send(sums[XC], stay, 1)
    total = total + send(sums[YS], across, 0)
    total = total + send(sums[YC], across, 1)
    total = total + send(sums[ZS], against, 0)
    total = total + send(sums[ZC], against, 1)
    return total.T


def solution(mesh):
    in_specs = (
        P(("groups", "ex"), None),
        P(("groups", "ex"), None),
        P(("groups", "ex")),
        P(("groups", "ex"), None),
    )
    out_specs = P(("groups", "ex"), None)
    return jax.shard_map(
        per_device, mesh=mesh, in_specs=in_specs, out_specs=out_specs, check_vma=False
    )
```

time: 511 us -> 175 us (0.34)
  Pallas kernels: 405 us -> 55.7 us
  waiting for transfers between devices: 15.5 us -> 79 us
  blocking collectives: 58 us -> 0 us
  starting transfers between devices: 13.6 us -> 30.1 us
  between operations: 11.3 us -> 0.09 us
    pallas_call x3, Pallas kernels: 389 us -> 42.1 us  [the longest x1 17.5 us: per_device(): pl.pallas_call(functools.partial(first_kernel, factor), in_specs=[smem, s...]
    ppermute x15 -> x20, waiting for transfers between devices: 15.5 us -> 79 us  [send(): return lax.ppermute(value, 'ex', pairs)]
    all_gather x1 -> x0, blocking collectives: 58 us -> none  [per_device(): every = lax.all_gather(info, 'ex')]
    ppermute x15 -> x20, starting transfers between devices: 13.6 us -> 30.1 us  [send(): return lax.ppermute(value, 'ex', pairs)]
    unnamed x8 -> x26, local copies, waits for them, and re-layouts: 1.25 us -> 7.73 us
  transfers between devices with their start and end apart: 15 -> 20, of which waited for: 4 -> 14; matrix products, arithmetic and copies ran while one was open for 1% -> 1% of each run, Pallas kernels for 76% -> 24%
where the time goes in v2:
time: 175 us; the launch traced here: 174 us
  waiting for transfers between devices  79 us (45%)
  Pallas kernels  55.7 us (32%)
  starting transfers between devices  30.1 us (17%)
  local copies, waits for them, and re-layouts  8.61 us (5%)
    ppermute x20, waiting for transfers between devices, send(): return lax.ppermute(value, 'ex', pairs)  79 us
    ppermute x20, starting transfers between devices, send(): return lax.ppermute(value, 'ex', pairs)  30.1 us
    pallas_call x1, Pallas kernels, per_device(): pl.pallas_call(functools.partial(first_kernel, factor), in_specs=[smem, s...  17.5 us
    pallas_call x1, Pallas kernels, grams(): pl.pallas_call(grams_kernel, in_specs=[pl.BlockSpec(memory_space=pltpu.SM...  13.6 us
    pallas_call x1, Pallas kernels, per_device(): pl.pallas_call(functools.partial(second_kernel, factor), in_specs=[smem,...  13.1 us
    pallas_call x1, Pallas kernels, cut(): pl.pallas_call(cut_kernel, grid_spec=pltpu.PrefetchScalarGridSpec(num_sca...  11.4 us
    unnamed x26, local copies, waits for them, and re-layouts  7.73 us
  transfers between devices with their start and end apart: 20, of which 14 were waited for; matrix products, arithmetic and copies ran while one was open for 1% of the time, Pallas kernels for 24%

profile of v2, /device:TPU:0, one launch (start us, length us, event | category | flops | bytes accessed | tf_op | source)
XLA Modules:
  0.0 174.2 jit_solution(2467297069837950625)
XLA Ops:
  0.0 3.0 %collective-permute-start.9 = (bf16[768,1024]{1,0:T(8,128)(2,1)}, bf16[768,1024]{1,0:T(8,128)(2,1)}, u32[]{:S(2)}, u32[]{:S(2)}) collective-permute-start(bf16[768,1024]{1,0:T(8,128)(2,1)} %xs.1), channel_id=1, source_target_pairs={{0,2},{1,3},{2,0},{3,1},{4,6},{5,7},{6,4},{7,5},{8,10},{9,11},{10,... | collective-permute-start | bytes 4718600 | tf_op jit(solution)/shard_map/ppermute | solution.py:51
  3.0 3.6 %collective-permute-start.11 = (bf16[768,1024]{1,0:T(8,128)(2,1)}, bf16[768,1024]{1,0:T(8,128)(2,1)}, u32[]{:S(2)}, u32[]{:S(2)}) collective-permute-start(bf16[768,1024]{1,0:T(8,128)(2,1)} %xs.1), channel_id=1, source_target_pairs={{0,12},{1,13},{2,6},{3,7},{4,0},{5,1},{6,10},{7,11},{8,4},{9,5},{1... | collective-permute-start | bytes 4718600 | tf_op jit(solution)/shard_map/ppermute | solution.py:51
  6.7 11.4 %cut.1 = (bf16[768,1280]{1,0:T(8,128)(2,1)}, bf16[768,1280]{1,0:T(8,128)(2,1)}, bf16[768,2560]{1,0:T(8,128)(2,1)}, bf16[768,1280]{1,0:T(8,128)(2,1)}, bf16[768,1280]{1,0:T(8,128)(2,1)}) custom-call(s32[5]{0:T(128)S(1)} %stack.51.places, bf16[768,5120]{1,0:T(8,128)(2,1)} %acts.3, bf16[768,5120]{1,0:T(8,128)(2,1)} %acts.3, bf16[768,5120]{1,0:T(8,128)(2,1)} %acts.3, ...), custom_call_target="tpu_custom_call" | custom-call | tf_op jit(solution)/shard_map/cut/pallas_call | solution.py:64
  18.6 19.1 %collective-permute-done.9.ys = bf16[768,1024]{1,0:T(8,128)(2,1)} collective-permute-done((bf16[768,1024]{1,0:T(8,128)(2,1)}, bf16[768,1024]{1,0:T(8,128)(2,1)}, u32[]{:S(2)}, u32[]{:S(2)}) %collective-permute-start.9) | collective-permute-done | bytes 1572896 | tf_op jit(solution)/shard_map/ppermute | solution.py:51
  37.7 2.6 %collective-permute-done.11.zs = bf16[768,1024]{1,0:T(8,128)(2,1)} collective-permute-done((bf16[768,1024]{1,0:T(8,128)(2,1)}, bf16[768,1024]{1,0:T(8,128)(2,1)}, u32[]{:S(2)}, u32[]{:S(2)}) %collective-permute-start.11) | collective-permute-done | bytes 1572896 | tf_op jit(solution)/shard_map/ppermute | solution.py:51
  40.9 2.4 %collective-permute-done = s32[1,128]{1,0:T(1,128)S(1)} collective-permute-done((s32[1,128]{1,0:T(1,128)S(1)}, s32[1,128]{1,0:T(1,128)S(1)}, u32[]{:S(2)}, u32[]{:S(2)}) %collective-permute-start) | collective-permute-done | bytes 544 | tf_op jit(solution)/shard_map/ppermute | solution.py:51
  43.3 1.4 collective-permute-start.1
  44.7 2.1 %collective-permute-done.1 = s32[1,128]{1,0:T(1,128)S(1)} collective-permute-done((s32[1,128]{1,0:T(1,128)S(1)}, s32[1,128]{1,0:T(1,128)S(1)}, u32[]{:S(2)}, u32[]{:S(2)}) %collective-permute-start.1) | collective-permute-done | bytes 544 | tf_op jit(solution)/shard_map/ppermute | solution.py:51
  47.0 2.8 %collective-permute-done.2 = s32[1,128]{1,0:T(1,128)S(1)} collective-permute-done((s32[1,128]{1,0:T(1,128)S(1)}, s32[1,128]{1,0:T(1,128)S(1)}, u32[]{:S(2)}, u32[]{:S(2)}) %collective-permute-start.2) | collective-permute-done | bytes 544 | tf_op jit(solution)/shard_map/ppermute | solution.py:51
  49.8 4.3 %collective-permute-start.3 = (s32[1,128]{1,0:T(1,128)S(1)}, s32[1,128]{1,0:T(1,128)S(1)}, u32[]{:S(2)}, u32[]{:S(2)}) collective-permute-start(s32[1,128]{1,0:T(1,128)S(1)} %add_bitcast_fusion.1), channel_id=1, source_target_pairs={{0,12},{1,13},{2,6},{3,7},{4,0},{5,1},{6,10},{7,11},{8,4},{9,5},{1... | collective-permute-start | bytes 1544 | tf_op jit(solution)/shard_map/ppermute | solution.py:51
  55.4 1.7 collective-permute-start.4
  58.4 3.0 %collective-permute-start.6 = (bf16[768,1280]{1,0:T(8,128)(2,1)}, bf16[768,1280]{1,0:T(8,128)(2,1)S(1)}, u32[]{:S(2)}, u32[]{:S(2)}) collective-permute-start(bf16[768,1280]{1,0:T(8,128)(2,1)} %get-tuple-element.17), channel_id=1, source_target_pairs={{0,2},{1,3},{2,0},{3,1},{4,6},{5,7},{6,4},{7,5},{8,10},{9,11},{10,... | collective-permute-start | bytes 5898248 | tf_op jit(solution)/shard_map/ppermute | solution.py:51
  62.5 2.9 %collective-permute-start.7 = (bf16[768,1280]{1,0:T(8,128)(2,1)}, bf16[768,1280]{1,0:T(8,128)(2,1)}, u32[]{:S(2)}, u32[]{:S(2)}) collective-permute-start(bf16[768,1280]{1,0:T(8,128)(2,1)} %get-tuple-element.18), channel_id=1, source_target_pairs={{0,12},{1,13},{2,6},{3,7},{4,0},{5,1},{6,10},{7,11},{8,4},{9,5},{1... | collective-permute-start | bytes 5898248 | tf_op jit(solution)/shard_map/ppermute | solution.py:51
  67.7 1.8 %collective-permute-start.14 = (bf16[768,1280]{1,0:T(8,128)(2,1)}, bf16[768,1280]{1,0:T(8,128)(2,1)}, u32[]{:S(2)}, u32[]{:S(2)}) collective-permute-start(bf16[768,1280]{1,0:T(8,128)(2,1)} %get-tuple-element.20), channel_id=1, source_target_pairs={{0,13},{1,12},{2,7},{3,6},{4,1},{5,0},{6,11},{7,10},{8,5},{9,4},{1... | collective-permute-start | bytes 5898248 | tf_op jit(solution)/shard_map/ppermute | solution.py:51
  74.5 13.6 %grams.1.gram = f32[7,768,768]{2,1,0:T(8,128)} custom-call(s32[6]{0:T(128)S(1)} %stack.45.flags, bf16[768,1024]{1,0:T(8,128)(2,1)S(1)} %copy-done, bf16[768,1024]{1,0:T(8,128)(2,1)S(1)} %copy-done.2, bf16[768,1024]{1,0:T(8,128)(2,1)} %collective-permute-done.9.ys, bf16[768,1024]{1,0:T(8,128)(2,1)S(1)} %copy-done.4, ...), custom_call_target="tpu_custom_call" | custom-call | flops 8455716864 | bytes 25952256 | tf_op jit(solution)/shard_map/grams/pallas_call | solution.py:114
  88.2 17.1 %collective-permute-done.6.ys = bf16[768,1280]{1,0:T(8,128)(2,1)S(1)} collective-permute-done((bf16[768,1280]{1,0:T(8,128)(2,1)}, bf16[768,1280]{1,0:T(8,128)(2,1)S(1)}, u32[]{:S(2)}, u32[]{:S(2)}) %collective-permute-start.6) | collective-permute-done | bytes 1966112 | tf_op jit(solution)/shard_map/ppermute | solution.py:51
  105.2 3.8 %collective-permute-done.7.zs = bf16[768,1280]{1,0:T(8,128)(2,1)} collective-permute-done((bf16[768,1280]{1,0:T(8,128)(2,1)}, bf16[768,1280]{1,0:T(8,128)(2,1)}, u32[]{:S(2)}, u32[]{:S(2)}) %collective-permute-start.7) | collective-permute-done | bytes 1966112 | tf_op jit(solution)/shard_map/ppermute | solution.py:51
  109.0 17.5 %first.1.earlier = f32[768,128]{1,0:T(8,128)S(1)} custom-call(s32[6]{0:T(128)S(1)} %stack.45.flags, s32[6,128]{1,0:T(8,128)S(1)} %concatenate.7.info.info_v, s32[6,128]{1,0:T(8,128)S(1)} %concatenate.7.info.info_v, bf16[768,5120]{1,0:T(8,128)(2,1)} %acts.3, bf16[768,2560]{1,0:T(8,128)(2,1)} %collective-permute-done.5.x_half, ...), custom_call_target="tpu_custom_call" | custom-call | flops 7549747200 | bytes 29097984 | tf_op jit(solution)/shard_map/first/pallas_call | solution.py:332
  126.5 20.9 %collective-permute-done.13.yc = bf16[768,1280]{1,0:T(8,128)(2,1)} collective-permute-done((bf16[768,1280]{1,0:T(8,128)(2,1)}, bf16[768,1280]{1,0:T(8,128)(2,1)}, u32[]{:S(2)}, u32[]{:S(2)}) %collective-permute-start.13) | collective-permute-done | bytes 1966112 | tf_op jit(solution)/shard_map/ppermute | solution.py:51
  148.1 13.1 %second.1 = (f32[48,96]{1,0:T(8,128)S(1)}, f32[48,96]{1,0:T(8,128)S(1)}, f32[48,96]{1,0:T(8,128)S(1)}, f32[48,96]{1,0:T(8,128)S(1)}, f32[48,96]{1,0:T(8,128)S(1)}, /*index=5*/f32[48,96]{1,0:T(8,128)S(1)}) custom-call(s32[6]{0:T(128)S(1)} %stack.45.flags, s32[6,128]{1,0:T(8,128)S(1)} %concatenate.7.info.info_v, s32[6,128]{1,0:T(8,128)S(1)} %concatenate.7.info.info_v, ...), custom_call_target="tpu_custom_call" | custom-call | flops 6039797760 | bytes 21233664 | tf_op jit(solution)/shard_map/second/pallas_call | solution.py:351
  161.3 4.3 %collective-permute-start.15 = (f32[48,96]{1,0:T(8,128)S(1)}, f32[48,96]{1,0:T(8,128)S(1)}, u32[]{:S(2)}, u32[]{:S(2)}) collective-permute-start(f32[48,96]{1,0:T(8,128)S(1)} %get-tuple-element.22), channel_id=1, source_target_pairs={{0,1},{1,0},{2,3},{3,2},{4,5},{5,4},{6,7},{7,6},{8,9},{9,8},{10,11... | collective-permute-start | bytes 55304 | tf_op jit(solution)/shard_map/ppermute | solution.py:51
  165.5 2.4 %collective-permute-start.16 = (f32[48,96]{1,0:T(8,128)S(1)}, f32[48,96]{1,0:T(8,128)S(1)}, u32[]{:S(2)}, u32[]{:S(2)}) collective-permute-start(f32[48,96]{1,0:T(8,128)S(1)} %get-tuple-element.23), channel_id=1, source_target_pairs={{0,2},{1,3},{2,0},{3,1},{4,6},{5,7},{6,4},{7,5},{8,10},{9,11},{10,... | collective-permute-start | bytes 55304 | tf_op jit(solution)/shard_map/ppermute | solution.py:51
  169.7 1.4 collective-permute-done.17
  171.2 2.4 %collective-permute-done.18 = f32[48,96]{1,0:T(8,128)S(1)} collective-permute-done((f32[48,96]{1,0:T(8,128)S(1)}, f32[48,96]{1,0:T(8,128)S(1)}, u32[]{:S(2)}, u32[]{:S(2)}) %collective-permute-start.18) | collective-permute-done | bytes 18464 | tf_op jit(solution)/shard_map/ppermute | solution.py:51
  (52 shorter events, 15.6 us)
Async XLA Ops:
  0.0 37.7 %collective-permute-start.9 = (bf16[768,1024]{1,0:T(8,128)(2,1)}, bf16[768,1024]{1,0:T(8,128)(2,1)}, u32[]{:S(2)}, u32[]{:S(2)}) collective-permute-start(bf16[768,1024]{1,0:T(8,128)(2,1)} %xs.1), channel_id=1, source_target_pairs={{0,2},{1,3},{2,0},{3,1},{4,6},{5,7},{6,4},{7,5},{8,10},{9,11},{10,... | collective-permute-start | bytes 4718600 | tf_op jit(solution)/shard_map/ppermute | solution.py:51
  3.0 37.3 %collective-permute-start.11 = (bf16[768,1024]{1,0:T(8,128)(2,1)}, bf16[768,1024]{1,0:T(8,128)(2,1)}, u32[]{:S(2)}, u32[]{:S(2)}) collective-permute-start(bf16[768,1024]{1,0:T(8,128)(2,1)} %xs.1), channel_id=1, source_target_pairs={{0,12},{1,13},{2,6},{3,7},{4,0},{5,1},{6,10},{7,11},{8,4},{9,5},{1... | collective-permute-start | bytes 4718600 | tf_op jit(solution)/shard_map/ppermute | solution.py:51
  6.7 33.6 %copy-start.11 = (s32[1,2]{1,0:T(1,128)S(1)}, s32[1,2]{1,0:T(1,128)}, u32[]{:S(2)}) copy-start(s32[1,2]{1,0:T(1,128)} %param.7) | copy-start | bytes 28
  6.7 33.6 %copy-start.12 = (s32[96]{0:T(128)S(1)}, s32[96]{0:T(128)}, u32[]{:S(2)}) copy-start(s32[96]{0:T(128)} %param.6) | copy-start | bytes 1156
  18.1 90.9 %collective-permute-start.5 = (bf16[768,2560]{1,0:T(8,128)(2,1)}, bf16[768,2560]{1,0:T(8,128)(2,1)}, u32[]{:S(2)}, u32[]{:S(2)}) collective-permute-start(bf16[768,2560]{1,0:T(8,128)(2,1)} %get-tuple-element.16), channel_id=1, source_target_pairs={{0,1},{1,0},{2,3},{3,2},{4,5},{5,4},{6,7},{7,6},{8,9},{9,8},{10,11... | collective-permute-start | bytes 11796488 | tf_op jit(solution)/shard_map/ppermute | solution.py:51
  18.1 43.2 %collective-permute-start.8 = (bf16[768,1024]{1,0:T(8,128)(2,1)S(1)}, bf16[768,1024]{1,0:T(8,128)(2,1)S(1)}, u32[]{:S(2)}, u32[]{:S(2)}) collective-permute-start(bf16[768,1024]{1,0:T(8,128)(2,1)S(1)} %copy-done), channel_id=1, source_target_pairs={{0,1},{1,0},{2,3},{3,2},{4,5},{5,4},{6,7},{7,6},{8,9},{9,8},{10,11... | collective-permute-start | bytes 4718600 | tf_op jit(solution)/shard_map/ppermute | solution.py:51
  37.7 27.7 %collective-permute-start.10 = (bf16[768,1024]{1,0:T(8,128)(2,1)}, bf16[768,1024]{1,0:T(8,128)(2,1)S(1)}, u32[]{:S(2)}, u32[]{:S(2)}) collective-permute-start(bf16[768,1024]{1,0:T(8,128)(2,1)} %collective-permute-done.9.ys), channel_id=1, source_target_pairs={{0,1},{1,0},{2,3},{3,2},{4,5},{5,4},{6,7},{7,6},{8,9},{9,8},{10,11... | collective-permute-start | bytes 4718600 | tf_op jit(solution)/shard_map/ppermute | solution.py:51
  40.3 26.3 %collective-permute-start.12 = (bf16[768,1024]{1,0:T(8,128)(2,1)}, bf16[768,1024]{1,0:T(8,128)(2,1)S(1)}, u32[]{:S(2)}, u32[]{:S(2)}) collective-permute-start(bf16[768,1024]{1,0:T(8,128)(2,1)} %collective-permute-done.11.zs), channel_id=1, source_target_pairs={{0,1},{1,0},{2,3},{3,2},{4,5},{5,4},{6,7},{7,6},{8,9},{9,8},{10,11... | collective-permute-start | bytes 4718600 | tf_op jit(solution)/shard_map/ppermute | solution.py:51
  40.3 3.0 %collective-permute-start = (s32[1,128]{1,0:T(1,128)S(1)}, s32[1,128]{1,0:T(1,128)S(1)}, u32[]{:S(2)}, u32[]{:S(2)}) collective-permute-start(s32[1,128]{1,0:T(1,128)S(1)} %add_bitcast_fusion.1), channel_id=1, source_target_pairs={{0,1},{1,0},{2,3},{3,2},{4,5},{5,4},{6,7},{7,6},{8,9},{9,8},{10,11... | collective-permute-start | bytes 1544 | tf_op jit(solution)/shard_map/ppermute | solution.py:51
  43.3 3.5 %collective-permute-start.1 = (s32[1,128]{1,0:T(1,128)S(1)}, s32[1,128]{1,0:T(1,128)S(1)}, u32[]{:S(2)}, u32[]{:S(2)}) collective-permute-start(s32[1,128]{1,0:T(1,128)S(1)} %add_bitcast_fusion.1), channel_id=1, source_target_pairs={{0,2},{1,3},{2,0},{3,1},{4,6},{5,7},{6,4},{7,5},{8,10},{9,11},{10,... | collective-permute-start | bytes 1544 | tf_op jit(solution)/shard_map/ppermute | solution.py:51
  46.8 19.7 %copy-start.7 = (s32[1,128]{1,0:T(1,128)}, s32[1,128]{1,0:T(1,128)S(1)}, u32[]{:S(2)}) copy-start(s32[1,128]{1,0:T(1,128)S(1)} %collective-permute-done.1) | copy-start | bytes 1540
  46.8 3.0 %collective-permute-start.2 = (s32[1,128]{1,0:T(1,128)S(1)}, s32[1,128]{1,0:T(1,128)S(1)}, u32[]{:S(2)}, u32[]{:S(2)}) collective-permute-start(s32[1,128]{1,0:T(1,128)S(1)} %add_bitcast_fusion.1), channel_id=1, source_target_pairs={{0,3},{1,2},{2,1},{3,0},{4,7},{5,6},{6,5},{7,4},{8,11},{9,10},{10,... | collective-permute-start | bytes 1544 | tf_op jit(solution)/shard_map/ppermute | solution.py:51
  49.8 17.9 %copy-start.8 = (s32[1,128]{1,0:T(1,128)}, s32[1,128]{1,0:T(1,128)S(1)}, u32[]{:S(2)}) copy-start(s32[1,128]{1,0:T(1,128)S(1)} %collective-permute-done.2) | copy-start | bytes 1540
  49.8 5.6 %collective-permute-start.3 = (s32[1,128]{1,0:T(1,128)S(1)}, s32[1,128]{1,0:T(1,128)S(1)}, u32[]{:S(2)}, u32[]{:S(2)}) collective-permute-start(s32[1,128]{1,0:T(1,128)S(1)} %add_bitcast_fusion.1), channel_id=1, source_target_pairs={{0,12},{1,13},{2,6},{3,7},{4,0},{5,1},{6,10},{7,11},{8,4},{9,5},{1... | collective-permute-start | bytes 1544 | tf_op jit(solution)/shard_map/ppermute | solution.py:51
  55.4 3.0 %collective-permute-start.4 = (s32[1,128]{1,0:T(1,128)S(1)}, s32[1,128]{1,0:T(1,128)S(1)}, u32[]{:S(2)}, u32[]{:S(2)}) collective-permute-start(s32[1,128]{1,0:T(1,128)S(1)} %add_bitcast_fusion.1), channel_id=1, source_target_pairs={{0,13},{1,12},{2,7},{3,6},{4,1},{5,0},{6,11},{7,10},{8,5},{9,4},{1... | collective-permute-start | bytes 1544 | tf_op jit(solution)/shard_map/ppermute | solution.py:51
  58.4 46.8 %collective-permute-start.6 = (bf16[768,1280]{1,0:T(8,128)(2,1)}, bf16[768,1280]{1,0:T(8,128)(2,1)S(1)}, u32[]{:S(2)}, u32[]{:S(2)}) collective-permute-start(bf16[768,1280]{1,0:T(8,128)(2,1)} %get-tuple-element.17), channel_id=1, source_target_pairs={{0,2},{1,3},{2,0},{3,1},{4,6},{5,7},{6,4},{7,5},{8,10},{9,11},{10,... | collective-permute-start | bytes 5898248 | tf_op jit(solution)/shard_map/ppermute | solution.py:51
  62.5 46.5 %collective-permute-start.7 = (bf16[768,1280]{1,0:T(8,128)(2,1)}, bf16[768,1280]{1,0:T(8,128)(2,1)}, u32[]{:S(2)}, u32[]{:S(2)}) collective-permute-start(bf16[768,1280]{1,0:T(8,128)(2,1)} %get-tuple-element.18), channel_id=1, source_target_pairs={{0,12},{1,13},{2,6},{3,7},{4,0},{5,1},{6,10},{7,11},{8,4},{9,5},{1... | collective-permute-start | bytes 5898248 | tf_op jit(solution)/shard_map/ppermute | solution.py:51
  66.5 80.9 %collective-permute-start.13 = (bf16[768,1280]{1,0:T(8,128)(2,1)}, bf16[768,1280]{1,0:T(8,128)(2,1)}, u32[]{:S(2)}, u32[]{:S(2)}) collective-permute-start(bf16[768,1280]{1,0:T(8,128)(2,1)} %get-tuple-element.19), channel_id=1, source_target_pairs={{0,3},{1,2},{2,1},{3,0},{4,7},{5,6},{6,5},{7,4},{8,11},{9,10},{10,... | collective-permute-start | bytes 5898248 | tf_op jit(solution)/shard_map/ppermute | solution.py:51
  67.7 80.4 %collective-permute-start.14 = (bf16[768,1280]{1,0:T(8,128)(2,1)}, bf16[768,1280]{1,0:T(8,128)(2,1)}, u32[]{:S(2)}, u32[]{:S(2)}) collective-permute-start(bf16[768,1280]{1,0:T(8,128)(2,1)} %get-tuple-element.20), channel_id=1, source_target_pairs={{0,13},{1,12},{2,7},{3,6},{4,1},{5,0},{6,11},{7,10},{8,5},{9,4},{1... | collective-permute-start | bytes 5898248 | tf_op jit(solution)/shard_map/ppermute | solution.py:51
  161.3 7.4 %collective-permute-start.15 = (f32[48,96]{1,0:T(8,128)S(1)}, f32[48,96]{1,0:T(8,128)S(1)}, u32[]{:S(2)}, u32[]{:S(2)}) collective-permute-start(f32[48,96]{1,0:T(8,128)S(1)} %get-tuple-element.22), channel_id=1, source_target_pairs={{0,1},{1,0},{2,3},{3,2},{4,5},{5,4},{6,7},{7,6},{8,9},{9,8},{10,11... | collective-permute-start | bytes 55304 | tf_op jit(solution)/shard_map/ppermute | solution.py:51
  165.5 4.2 %collective-permute-start.16 = (f32[48,96]{1,0:T(8,128)S(1)}, f32[48,96]{1,0:T(8,128)S(1)}, u32[]{:S(2)}, u32[]{:S(2)}) collective-permute-start(f32[48,96]{1,0:T(8,128)S(1)} %get-tuple-element.23), channel_id=1, source_target_pairs={{0,2},{1,3},{2,0},{3,1},{4,6},{5,7},{6,4},{7,5},{8,10},{9,11},{10,... | collective-permute-start | bytes 55304 | tf_op jit(solution)/shard_map/ppermute | solution.py:51
  167.9 3.3 %collective-permute-start.17 = (f32[48,96]{1,0:T(8,128)S(1)}, f32[48,96]{1,0:T(8,128)S(1)}, u32[]{:S(2)}, u32[]{:S(2)}) collective-permute-start(f32[48,96]{1,0:T(8,128)S(1)} %get-tuple-element.24), channel_id=1, source_target_pairs={{0,3},{1,2},{2,1},{3,0},{4,7},{5,6},{6,5},{7,4},{8,11},{9,10},{10,... | collective-permute-start | bytes 55304 | tf_op jit(solution)/shard_map/ppermute | solution.py:51
  168.0 5.6 %collective-permute-start.18 = (f32[48,96]{1,0:T(8,128)S(1)}, f32[48,96]{1,0:T(8,128)S(1)}, u32[]{:S(2)}, u32[]{:S(2)}) collective-permute-start(f32[48,96]{1,0:T(8,128)S(1)} %get-tuple-element.25), channel_id=1, source_target_pairs={{0,4},{1,5},{2,14},{3,15},{4,8},{5,9},{6,2},{7,3},{8,12},{9,13},{1... | collective-permute-start | bytes 55304 | tf_op jit(solution)/shard_map/ppermute | solution.py:51
  168.0 5.6 %collective-permute-start.19 = (f32[48,96]{1,0:T(8,128)S(1)}, f32[48,96]{1,0:T(8,128)S(1)}, u32[]{:S(2)}, u32[]{:S(2)}) collective-permute-start(f32[48,96]{1,0:T(8,128)S(1)} %get-tuple-element.26), channel_id=1, source_target_pairs={{0,5},{1,4},{2,15},{3,14},{4,9},{5,8},{6,3},{7,2},{8,13},{9,12},{1... | collective-permute-start | bytes 55304 | tf_op jit(solution)/shard_map/ppermute | solution.py:51
  (9 other events, 40.8 us)

commit v3 on v2

v3 whole, which is shorter than its diff:
```python
import functools
import math

import jax
import jax.numpy as jnp
from jax import lax
from jax.experimental import pallas as pl
from jax.experimental.pallas import tpu as pltpu
from jax.sharding import PartitionSpec as P

TOK = 8
DOMAINS = 48
LANES = 128
VMEM_BYTES = 40 * 1024 * 1024
CUT_VMEM_BYTES = 60 * 1024 * 1024

INFO = 16

XS, XC, YS, YC, ZS, ZC = range(6)
PAIRS = (
    (YS, XS, 1), (YS, ZS, 1), (YS, XC, 0), (XC, XS, 0),
    (YC, XC, 1), (YC, ZC, 1), (YC, ZS, 0), (YS, ZC, 0), (YC, XS, 0),
)
ONLY = {2: 0, 6: 0, 7: 1, 8: 1}
SLOT = (0, 1, 2, 3, 4, 5, 6, 6, 2)
FIRST = (0, 1, 2, 3)
SECOND = (4, 5, 6, 7, 8)
SMALL = pl.CostEstimate(flops=1, bytes_accessed=1, transcendentals=0)
NT = (((1,), (1,)), ((), ()))


def across(chip):
    return chip ^ 1


def along(chip):
    return chip + 2 if chip & 1 else chip - 2


def against(chip):
    return chip - 2 if chip & 1 else chip + 2


def stay(chip):
    return chip


def send(value, move, flip):
    chips = lax.axis_size("ex") // 2
    pairs = [
        (2 * chip + core, 2 * (move(chip) % chips) + (core ^ flip))
        for chip in range(chips)
        for core in range(2)
    ]
    return lax.ppermute(value, "ex", pairs)


def token_major(rows):
    to = lax.broadcasted_iota(jnp.int32, (rows, rows), 0)
    source = lax.broadcasted_iota(jnp.int32, (rows, rows), 1)
    examples = rows // TOK
    return ((source % TOK) * examples + source // TOK == to).astype(jnp.bfloat16)


def reorder(order, block):
    return jnp.dot(order, block, preferred_element_type=jnp.float32).astype(jnp.bfloat16)


def put(target, value, info):
    rows = value.shape[0]
    target[:rows, :] = value
    target[rows:, :] = jnp.concatenate([info[...]] * (target.shape[1] // LANES), axis=1)


def cut_kernel(steps, places, info, y_acts, z_acts, grads, y_out, z_out, order):
    step = pl.program_id(0)

    @pl.when(step == 0)
    def _():
        order[...] = token_major(order.shape[0])

    @pl.when(step < steps)
    def _():
        put(y_out, reorder(order[...], y_acts[...]), info)
        put(z_out, z_acts[...], info)

    @pl.when(step >= steps)
    def _():
        put(y_out, reorder(order[...], grads[...]), info)
        put(z_out, grads[...], info)


def cut(acts, grads, info, places, with_grads):
    rows, width = acts.shape
    quarter, depth = width // 4, grads.shape[1]
    step = math.gcd(math.gcd(quarter, depth), 256)
    steps = quarter // step
    more = depth // step if with_grads else 0
    block = (rows, step)
    return pl.pallas_call(
        functools.partial(cut_kernel, steps),
        grid_spec=pltpu.PrefetchScalarGridSpec(
            num_scalar_prefetch=1,
            grid=(steps + more,),
            in_specs=[
                pl.BlockSpec((INFO, LANES), lambda i, p: (0, 0)),
                pl.BlockSpec(block, lambda i, p: (0, p[0] * steps + jnp.minimum(i, steps - 1))),
                pl.BlockSpec(block, lambda i, p: (0, p[1] * steps + jnp.minimum(i, steps - 1))),
                pl.BlockSpec(block, lambda i, p: (0, jnp.maximum(i - steps, 0))),
            ],
            out_specs=[pl.BlockSpec((rows + INFO, step), lambda i, p: (0, i))] * 2,
            scratch_shapes=[pltpu.VMEM((rows, rows), jnp.bfloat16)],
        ),
        out_shape=[
            jax.ShapeDtypeStruct((rows + INFO, quarter + more * step), acts.dtype)
        ] * 2,
        compiler_params=pltpu.CompilerParams(vmem_limit_bytes=CUT_VMEM_BYTES),
        cost_estimate=SMALL,
        name="cut",
    )(places, info, acts, acts, grads)


def half_kernel(steps, place, info, acts, grads, out):
    @pl.when(pl.program_id(0) < steps)
    def _():
        put(out, acts[...], info)

    @pl.when(pl.program_id(0) >= steps)
    def _():
        put(out, grads[...], info)


def cut_half(acts, grads, info, place):
    rows, width = acts.shape
    half, depth = width // 2, grads.shape[1]
    step = math.gcd(math.gcd(half, depth), 512)
    steps = half // step
    return pl.pallas_call(
        functools.partial(half_kernel, steps),
        grid_spec=pltpu.PrefetchScalarGridSpec(
            num_scalar_prefetch=1,
            grid=(steps + depth // step,),
            in_specs=[
                pl.BlockSpec((INFO, LANES), lambda i, p: (0, 0)),
                pl.BlockSpec((rows, step), lambda i, p: (0, p[0] * steps + jnp.minimum(i, steps - 1))),
                pl.BlockSpec((rows, step), lambda i, p: (0, jnp.maximum(i - steps, 0))),
            ],
            out_specs=pl.BlockSpec((rows + INFO, step), lambda i, p: (0, i)),
        ),
        out_shape=jax.ShapeDtypeStruct((rows + INFO, half + depth), acts.dtype),
        compiler_params=pltpu.CompilerParams(vmem_limit_bytes=CUT_VMEM_BYTES),
        cost_estimate=SMALL,
        name="half",
    )(place, info, acts, grads)


def guarded(pair, mirrored, work):
    if pair in ONLY:
        pl.when(mirrored == ONLY[pair])(work)
    else:
        work()


def grams_kernel(flags, xs, xc, ys, yc, zs, zc, out, held, result, in_sems, out_sems):
    mirrored = flags[0]
    rows, depth = xs.shape
    sources = [xs] + [
        message.at[:rows, message.shape[1] - depth:] for message in (xc, ys, yc, zs, zc)
    ]
    loads = [
        pltpu.make_async_copy(source, held.at[at], in_sems.at[at])
        for at, source in enumerate(sources)
    ]
    for load in loads:
        load.start()
    for load in loads:
        load.wait()
    for pair, (one, two, _) in enumerate(PAIRS):
        slot = SLOT[pair]

        def work(one=one, two=two, slot=slot):
            result[slot] = lax.dot_general(
                held[one], held[two], NT, preferred_element_type=jnp.float32
            )
            pltpu.make_async_copy(result.at[slot], out.at[slot], out_sems.at[slot]).start()

        guarded(pair, mirrored, work)
    for slot in range(7):
        pltpu.make_async_copy(result.at[slot], out.at[slot], out_sems.at[slot]).wait()


def grams(flags, grads, *messages):
    rows, width = grads.shape
    return pl.pallas_call(
        grams_kernel,
        in_specs=[pl.BlockSpec(memory_space=pltpu.SMEM)] + [pl.BlockSpec(memory_space=pl.ANY)] * 6,
        out_specs=pl.BlockSpec(memory_space=pl.ANY),
        out_shape=jax.ShapeDtypeStruct((7, rows, rows), jnp.float32),
        scratch_shapes=[
            pltpu.VMEM((6, rows, width), grads.dtype),
            pltpu.VMEM((7, rows, rows), jnp.float32),
            pltpu.SemaphoreType.DMA((6,)),
            pltpu.SemaphoreType.DMA((7,)),
        ],
        compiler_params=pltpu.CompilerParams(vmem_limit_bytes=VMEM_BYTES),
        cost_estimate=SMALL,
        name="grams",
    )(flags, grads, *messages)


def token_sums(one, two, gram, sums, ordered=True):
    examples, rows = sums.shape
    step = math.gcd(rows, 256)
    for at in range(0, rows, step):
        cols = slice(at, at + step)
        inner = lax.dot_general(
            one[:rows, :], two[cols, :], NT, preferred_element_type=jnp.float32
        )
        weighted = inner * gram[:, cols]
        if ordered:
            total = weighted[:examples]
            for token in range(1, TOK):
                total = total + weighted[token * examples:(token + 1) * examples]
        else:
            total = weighted.reshape(examples, TOK, step).sum(axis=1)
        sums[:, cols] = total


def two_parts(value):
    high = value.astype(jnp.bfloat16)
    return high, (value - high.astype(jnp.float32)).astype(jnp.bfloat16)


def dot_parts(value, table):
    high, low = two_parts(value)
    return lax.dot_general(low, table, NT, preferred_element_type=jnp.float32) + lax.dot_general(
        high, table, NT, preferred_element_type=jnp.float32
    )


def domain_sums(pairs, factor, flags, info, sums, table):
    count, examples, rows = sums.shape
    example = lax.broadcasted_iota(jnp.int32, (LANES, rows), 0)
    gather = (lax.broadcasted_iota(jnp.int32, (LANES, rows), 1) // TOK == example)
    tiles = dot_parts(sums[...].reshape(count * examples, rows), gather.astype(jnp.bfloat16))
    tiles = tiles.reshape(count, examples, LANES)
    core, side = flags[3], flags[4]
    lane = lax.broadcasted_iota(jnp.int32, (1, LANES), 1)

    def listed_flag(block, apart):
        return jnp.sum(jnp.where(lane == examples + apart, info[block], 0.0), axis=1, keepdims=True)

    table[...] = jnp.zeros_like(table)
    pad = jnp.zeros((LANES - examples, LANES), jnp.float32)
    for at, pair in enumerate(pairs):
        one, two, apart = PAIRS[pair]
        if one == XC:
            two_leads = core == 0
        elif two in (XS, XC):
            two_leads = side == 0
        else:
            two_leads = side == 1
        flag = jnp.where(two_leads, listed_flag(two, apart), listed_flag(one, apart))
        tile = jnp.concatenate([tiles[at], pad], axis=0) * (flag * factor)
        table[one * LANES:(one + 1) * LANES, two * LANES:(two + 1) * LANES] = tile
        table[two * LANES:(two + 1) * LANES, one * LANES:(one + 1) * LANES] = tile.T
    row = lax.broadcasted_iota(jnp.int32, (LANES, LANES), 0)
    hot = jnp.concatenate(
        [
            ((info[block].astype(jnp.int32) == row) & (lane < examples)).astype(jnp.bfloat16)
            if block in info else jnp.zeros((LANES, LANES), jnp.bfloat16)
            for block in range(6)
        ],
        axis=1,
    )
    return dot_parts(table[...], hot)


def staged(loads, sems, plan):
    copies = {
        key: pltpu.make_async_copy(source, target, sems.at[at])
        for at, (key, (source, target)) in enumerate(loads.items())
    }

    def start(at):
        if at < len(plan):
            for key in plan[at][0]:
                copies[key].start()

    def ready(at):
        if at == 0:
            start(0)
        for key in plan[at][0]:
            copies[key].wait()
        start(at + 1)

    return ready


def info_row(message, rows):
    return message[rows:rows + INFO, :LANES].astype(jnp.float32)[:1]


def first_kernel(factor, flags, xs, acts, x_half, ys, zs, gram, out,
                 xs_v, xc_v, ys_v, zs_v, own_v, half_v, gram_v, sums, table, sems):
    mirrored, half_at, in_half = flags[0], flags[1], flags[2]
    quarter = xs_v.shape[1]
    loads = {
        "xs": (xs.at[:, :quarter], xs_v),
        "ys": (ys.at[:, :quarter], ys_v),
        "g0": (gram.at[0], gram_v.at[0]),
        "zs": (zs.at[:, :quarter], zs_v),
        "g1": (gram.at[1], gram_v.at[1]),
        "xc": (x_half.at[:, pl.ds(pl.multiple_of(in_half, LANES), quarter)], xc_v),
        "g2": (gram.at[2], gram_v.at[2]),
        "own": (acts.at[:, pl.ds(pl.multiple_of(half_at, LANES), 2 * quarter)], own_v),
        "half": (x_half.at[:, :2 * quarter], half_v),
        "g3": (gram.at[3], gram_v.at[3]),
    }
    plan = (
        (("xs", "ys", "g0"), ys_v, xs_v),
        (("zs", "g1"), ys_v, zs_v),
        (("xc", "g2"), ys_v, xc_v),
        (("own", "half", "g3"), half_v, own_v),
    )
    ready = staged(loads, sems, plan)
    for at, pair in enumerate(FIRST):
        _, one, two = plan[at]
        ready(at)
        if pair in ONLY:
            sums[at] = jnp.zeros(sums.shape[1:], jnp.float32)
        guarded(pair, mirrored, functools.partial(
            token_sums, one, two, gram_v.at[at], sums.at[at], PAIRS[pair][0] != XC))
    rows = sums.shape[2]
    info = {XS: info_row(xs_v, rows), XC: info_row(xc_v, rows),
            YS: info_row(ys_v, rows), ZS: info_row(zs_v, rows)}
    out[...] = domain_sums(FIRST, factor, flags, info, sums, table)


def second_kernel(factor, flags, earlier, xs, x_half, ys, yc, zs, zc, gram, *rest):
    outs = rest[:6]
    xs_v, xc_v, ys_v, yc_v, zs_v, zc_v, gram_v, sums, table, sems = rest[6:]
    mirrored, in_half = flags[0], flags[2]
    quarter = xs_v.shape[1]
    loads = {
        "yc": (yc, yc_v),
        "xc": (x_half.at[:, pl.ds(pl.multiple_of(in_half, LANES), quarter)], xc_v),
        "g4": (gram.at[4], gram_v.at[0]),
        "zc": (zc, zc_v),
        "g5": (gram.at[5], gram_v.at[1]),
        "ys": (ys.at[:, :quarter], ys_v),
        "zs": (zs.at[:, :quarter], zs_v),
        "g6": (gram.at[6], gram_v.at[2]),
        "xs": (xs.at[:, :quarter], xs_v),
        "g2": (gram.at[2], gram_v.at[3]),
    }
    plan = (
        (("yc", "xc", "g4"), yc_v, xc_v, 0),
        (("zc", "g5"), yc_v, zc_v, 1),
        (("ys", "zs", "g6"), yc_v, zs_v, 2),
        (("xs", "g2"), ys_v, zc_v, 2),
        ((), yc_v, xs_v, 3),
    )
    ready = staged(loads, sems, plan)
    for at, pair in enumerate(SECOND):
        _, one, two, slot = plan[at]
        ready(at)
        if pair in ONLY:
            sums[at] = jnp.zeros(sums.shape[1:], jnp.float32)
        guarded(pair, mirrored, functools.partial(token_sums, one, two, gram_v.at[slot], sums.at[at]))
    examples, rows = sums.shape[1:]
    info = {
        block: info_row(message, rows)
        for block, message in enumerate((xs_v, xc_v, ys_v, yc_v, zs_v, zc_v))
    }
    total = (earlier[...] + domain_sums(SECOND, factor, flags, info, sums, table)).T
    for block, out in enumerate(outs):
        out[...] = total[:DOMAINS, block * LANES:block * LANES + examples]


def per_device(acts, grads, domain, listed):
    rows, width = acts.shape
    examples = rows // TOK
    quarter = width // 4
    me = lax.axis_index("ex")
    core = me % 2
    side = (me // 2) % 2
    mirrored = core ^ side

    flags = jnp.stack([
        mirrored, core * 2 * quarter, (1 - side) * quarter, core, side
    ]).astype(jnp.int32)
    places = jnp.stack([core * 2 + side, core * 2 + (1 - side)]).astype(jnp.int32)
    cross_places = jnp.stack([(1 - core) * 2 + side, (1 - core) * 2 + (1 - side)]).astype(jnp.int32)
    half_place = jnp.stack([1 - core]).astype(jnp.int32)

    own_info = jnp.concatenate(
        [domain, listed[0], jnp.zeros((LANES - examples - 2,), jnp.int32)]
    )
    own_info = jnp.broadcast_to(own_info.astype(acts.dtype)[None, :], (INFO, LANES))

    cut_ys, cut_zs = cut(acts, grads, own_info, places, True)
    ys = send(cut_ys, across, 0)
    zs = send(cut_zs, along, 0)
    own_info, _ = lax.optimization_barrier((own_info, cut_ys))
    x_half = send(cut_half(acts, grads, own_info, half_place), stay, 1)
    cut_yc, cut_zc = cut(acts, grads, own_info, cross_places, False)
    yc = send(cut_yc, across, 1)
    zc = send(cut_zc, along, 1)
    grads_yc = send(ys[:, quarter:], stay, 1)
    grads_zc = send(zs[:, quarter:], stay, 1)
    factor = 1.0 / (TOK * math.sqrt(width * grads.shape[1]))

    gram = grams(flags, grads, x_half, ys, grads_yc, zs, grads_zc)

    smem = pl.BlockSpec(memory_space=pltpu.SMEM)
    vmem = pl.BlockSpec(memory_space=pltpu.VMEM)
    hbm = pl.BlockSpec(memory_space=pl.ANY)
    params = pltpu.CompilerParams(vmem_limit_bytes=VMEM_BYTES)
    slice_v = pltpu.VMEM((rows + INFO, quarter), acts.dtype)
    half_v = pltpu.VMEM((rows + INFO, 2 * quarter), acts.dtype)
    own_v = pltpu.VMEM((rows, 2 * quarter), acts.dtype)
    gram_v = pltpu.VMEM((4, rows, rows), jnp.float32)
    table_v = pltpu.VMEM((6 * LANES, 6 * LANES), jnp.float32)
    first = pl.pallas_call(
        functools.partial(first_kernel, factor),
        in_specs=[smem] + [hbm] * 6,
        out_specs=vmem,
        out_shape=jax.ShapeDtypeStruct((6 * LANES, LANES), jnp.float32),
        scratch_shapes=[slice_v] * 4 + [own_v, half_v] + [
            gram_v,
            pltpu.VMEM((4, examples, rows), jnp.float32),
            table_v,
            pltpu.SemaphoreType.DMA((10,)),
        ],
        compiler_params=params,
        cost_estimate=SMALL,
        name="first",
    )(flags, cut_zs, acts, x_half, ys, zs, gram)
    sums = pl.pallas_call(
        functools.partial(second_kernel, factor),
        in_specs=[smem, vmem] + [hbm] * 7,
        out_specs=[vmem] * 6,
        out_shape=[jax.ShapeDtypeStruct((DOMAINS, examples), jnp.float32)] * 6,
        scratch_shapes=[slice_v] * 6 + [
            gram_v,
            pltpu.VMEM((5, examples, rows), jnp.float32),
            table_v,
            pltpu.SemaphoreType.DMA((10,)),
        ],
        compiler_params=params,
        cost_estimate=SMALL,
        name="second",
    )(flags, first, cut_zs, x_half, ys, yc, zs, zc, gram)

    total = sums[XS]
    total = total + send(sums[XC], stay, 1)
    total = total + send(sums[YS], across, 0)
    total = total + send(sums[YC], across, 1)
    total = total + send(sums[ZS], against, 0)
    total = total + send(sums[ZC], against, 1)
    return total.T


def solution(mesh):
    in_specs = (
        P(("groups", "ex"), None),
        P(("groups", "ex"), None),
        P(("groups", "ex")),
        P(("groups", "ex"), None),
    )
    out_specs = P(("groups", "ex"), None)
    return jax.shard_map(
        per_device, mesh=mesh, in_specs=in_specs, out_specs=out_specs, check_vma=False
    )
```

time: 175 us -> 173 us (0.989)
  starting transfers between devices: 30.1 us -> 13.4 us
  Pallas kernels: 55.7 us -> 71.5 us
  other arithmetic: 0.7 us -> 3.33 us
  local copies, waits for them, and re-layouts: 8.61 us -> 6.32 us
    ppermute x20 -> x12, starting transfers between devices: 30.1 us -> 13.4 us  [send(): return lax.ppermute(value, 'ex', pairs)]
    pallas_call x2 -> x4, Pallas kernels: 28.9 us -> 44.1 us  [the longest x2 18.4 us: cut(): pl.pallas_call(functools.partial(cut_kernel, steps), grid_spec=pltpu.Pref...]
    unnamed x26 -> x2, local copies, waits for them, and re-layouts: 7.73 us -> 0.01 us
    slice x0 -> x2, local copies, waits for them, and re-layouts: none -> 5.63 us  [the longest x1 2.9 us: per_device(): grads_zc = send(zs[:, quarter:], stay, 1)]
    another operation x0 -> x3, other arithmetic: none -> 1.97 us  [the longest x1 0.67 us: per_device(): jnp.stack([(1 - core) * 2 + side, (1 - core) * 2 + (1 - side)])]
    ppermute x20 -> x12, waiting for transfers between devices: 79 us -> 78 us  [send(): return lax.ppermute(value, 'ex', pairs)]
  transfers between devices with their start and end apart: 20 -> 12, of which waited for: 14 -> 8; matrix products, arithmetic and copies ran while one was open for 1% -> 4% of each run, Pallas kernels for 24% -> 23%
where the time goes in v3:
time: 173 us
  waiting for transfers between devices  78 us (45%)
  Pallas kernels  71.5 us (41%)
  starting transfers between devices  13.4 us (8%)
  local copies, waits for them, and re-layouts  6.32 us (4%)
  other arithmetic  3.33 us (2%)
    ppermute x12, waiting for transfers between devices, send(): return lax.ppermute(value, 'ex', pairs)  78 us
    pallas_call x2, Pallas kernels, cut(): pl.pallas_call(functools.partial(cut_kernel, steps), grid_spec=pltpu.Pref...  18.4 us
    pallas_call x1, Pallas kernels, per_device(): pl.pallas_call(functools.partial(first_kernel, factor), in_specs=[smem] +...  17.8 us
    pallas_call x1, Pallas kernels, grams(): pl.pallas_call(grams_kernel, in_specs=[pl.BlockSpec(memory_space=pltpu.SM...  14.5 us
    ppermute x12, starting transfers between devices, send(): return lax.ppermute(value, 'ex', pairs)  13.4 us
    pallas_call x1, Pallas kernels, per_device(): pl.pallas_call(functools.partial(second_kernel, factor), in_specs=[smem,...  13 us
    pallas_call x1, Pallas kernels, cut_half(): pl.pallas_call(functools.partial(half_kernel, steps), grid_spec=pltpu.Pre...  7.88 us
  transfers between devices with their start and end apart: 12, of which 8 were waited for; matrix products, arithmetic and copies ran while one was open for 4% of the time, Pallas kernels for 23%

profile of v3, /device:TPU:0, one launch (start us, length us, event | category | flops | bytes accessed | tf_op | source)
XLA Modules:
  0.0 172.6 jit_solution(2612681822250938317)
XLA Ops:
  0.0 0.7 convert.9
  0.7 0.7 convert_bitcast_fusion
  1.3 0.6 pad_add_fusion.places
  2.0 0.6 broadcast_in_dim.2.info
  2.6 11.0 %cut.2 = (bf16[784,2304]{1,0:T(8,128)(2,1)}, bf16[784,2304]{1,0:T(8,128)(2,1)}) custom-call(s32[2]{0:T(128)} %pad_add_fusion.places, bf16[16,128]{1,0:T(8,128)(2,1)} %broadcast_in_dim.2.info, bf16[768,5120]{1,0:T(8,128)(2,1)} %z_acts.3, bf16[768,5120]{1,0:T(8,128)(2,1)} %z_acts.3, bf16[768,1024]{1,0:T(8,128)(2,1)} %grads.5), custom_call_target="tpu_custom_call" | custom-call | flops 1 | bytes 1 | tf_op jit(solution)/shard_map/cut/pallas_call | solution.py:100
  13.7 7.9 %half.1 = bf16[784,3584]{1,0:T(8,128)(2,1)} custom-call(s32[1]{0:T(128)} %bitcast.8.place, bf16[16,128]{1,0:T(8,128)(2,1)} %broadcast_in_dim.2.info, bf16[768,5120]{1,0:T(8,128)(2,1)} %z_acts.3, bf16[768,1024]{1,0:T(8,128)(2,1)} %grads.5), custom_call_target="tpu_custom_call" | custom-call | flops 1 | bytes 1 | tf_op jit(solution)/shard_map/half/pallas_call | solution.py:138
  22.0 2.5 %collective-permute-start.1 = (bf16[784,2304]{1,0:T(8,128)(2,1)}, bf16[784,2304]{1,0:T(8,128)(2,1)}, u32[]{:S(2)}, u32[]{:S(2)}) collective-permute-start(bf16[784,2304]{1,0:T(8,128)(2,1)} %get-tuple-element.17), channel_id=1, source_target_pairs={{0,2},{1,3},{2,0},{3,1},{4,6},{5,7},{6,4},{7,5},{8,10},{9,11},{10,... | collective-permute-start | bytes 10838024 | tf_op jit(solution)/shard_map/ppermute | solution.py:55
  24.5 3.6 %collective-permute-start.2 = (bf16[784,2304]{1,0:T(8,128)(2,1)}, bf16[784,2304]{1,0:T(8,128)(2,1)}, u32[]{:S(2)}, u32[]{:S(2)}) collective-permute-start(bf16[784,2304]{1,0:T(8,128)(2,1)} %get-tuple-element.16.xs), channel_id=1, source_target_pairs={{0,12},{1,13},{2,6},{3,7},{4,0},{5,1},{6,10},{7,11},{8,4},{9,5},{1... | collective-permute-start | bytes 10838024 | tf_op jit(solution)/shard_map/ppermute | solution.py:55
  28.1 0.7 pad_add_fusion.1.places
  28.8 7.4 %cut.3 = (bf16[784,1280]{1,0:T(8,128)(2,1)}, bf16[784,1280]{1,0:T(8,128)(2,1)}) custom-call(s32[2]{0:T(128)} %pad_add_fusion.1.places, bf16[16,128]{1,0:T(8,128)(2,1)} %broadcast_in_dim.2.info, bf16[768,5120]{1,0:T(8,128)(2,1)} %z_acts.3, bf16[768,5120]{1,0:T(8,128)(2,1)} %z_acts.3, bf16[768,1024]{1,0:T(8,128)(2,1)} %grads.5), custom_call_target="tpu_custom_call" | custom-call | flops 1 | bytes 1 | tf_op jit(solution)/shard_map/cut/pallas_call | solution.py:100
  36.4 67.3 %collective-permute-done.1.ys = bf16[784,2304]{1,0:T(8,128)(2,1)} collective-permute-done((bf16[784,2304]{1,0:T(8,128)(2,1)}, bf16[784,2304]{1,0:T(8,128)(2,1)}, u32[]{:S(2)}, u32[]{:S(2)}) %collective-permute-start.1) | collective-permute-done | bytes 3612704 | tf_op jit(solution)/shard_map/ppermute | solution.py:55
  103.8 2.7 %slice.8 = bf16[784,1024]{1,0:T(8,128)(2,1)} slice(bf16[784,2304]{1,0:T(8,128)(2,1)} %collective-permute-done.1.ys), slice={[0:784], [1280:2304]} | slice | bytes 3211264 | tf_op jit(solution)/shard_map/slice | solution.py:410
  106.9 2.9 %slice.9 = bf16[784,1024]{1,0:T(8,128)(2,1)} slice(bf16[784,2304]{1,0:T(8,128)(2,1)} %collective-permute-done.2.zs), slice={[0:784], [1280:2304]} | slice | bytes 3211264 | tf_op jit(solution)/shard_map/slice | solution.py:411
  110.2 3.4 %collective-permute-done.4.zc = bf16[784,1024]{1,0:T(8,128)(2,1)} collective-permute-done((bf16[784,1024]{1,0:T(8,128)(2,1)}, bf16[784,1024]{1,0:T(8,128)(2,1)}, u32[]{:S(2)}, u32[]{:S(2)}) %collective-permute-start.4) | collective-permute-done | bytes 1605664 | tf_op jit(solution)/shard_map/ppermute | solution.py:55
  113.6 14.5 %grams.1.gram = f32[7,768,768]{2,1,0:T(8,128)} custom-call(s32[5]{0:T(128)S(1)} %stack.44.flags, bf16[768,1024]{1,0:T(8,128)(2,1)S(1)} %copy-done, bf16[784,3584]{1,0:T(8,128)(2,1)} %collective-permute-done.xc.x_half, bf16[784,2304]{1,0:T(8,128)(2,1)} %collective-permute-done.1.ys, bf16[784,1024]{1,0:T(8,128)(2,1)S(1)} %collective-permute-done.3.yc, ...), custom_call_target="tpu_custom_call" | custom-call | flops 1 | bytes 1 | tf_op jit(solution)/shard_map/grams/pallas_call | solution.py:194
  128.1 17.8 %first.1.earlier = f32[768,128]{1,0:T(8,128)S(1)} custom-call(s32[5]{0:T(128)S(1)} %stack.44.flags, bf16[784,2304]{1,0:T(8,128)(2,1)} %get-tuple-element.16.xs, bf16[768,5120]{1,0:T(8,128)(2,1)} %z_acts.3, bf16[784,3584]{1,0:T(8,128)(2,1)} %collective-permute-done.xc.x_half, bf16[784,2304]{1,0:T(8,128)(2,1)} %collective-permute-done.1.ys, ...), custom_call_target="tpu_custom_call" | custom-call | flops 1 | bytes 1 | tf_op jit(solution)/shard_map/first/pallas_call | solution.py:425
  145.9 0.5 collective-permute-done.5.yc
  146.4 2.8 %collective-permute-done.6.zc = bf16[784,1280]{1,0:T(8,128)(2,1)} collective-permute-done((bf16[784,1280]{1,0:T(8,128)(2,1)}, bf16[784,1280]{1,0:T(8,128)(2,1)}, u32[]{:S(2)}, u32[]{:S(2)}) %collective-permute-start.6) | collective-permute-done | bytes 2007072 | tf_op jit(solution)/shard_map/ppermute | solution.py:55
  149.2 13.0 %second.1 = (f32[48,96]{1,0:T(8,128)S(1)}, f32[48,96]{1,0:T(8,128)S(1)}, f32[48,96]{1,0:T(8,128)S(1)}, f32[48,96]{1,0:T(8,128)S(1)}, f32[48,96]{1,0:T(8,128)S(1)}, /*index=5*/f32[48,96]{1,0:T(8,128)S(1)}) custom-call(s32[5]{0:T(128)S(1)} %stack.44.flags, f32[768,128]{1,0:T(8,128)S(1)} %first.1.earlier, bf16[784,2304]{1,0:T(8,128)(2,1)} %get-tuple-element.16.xs, ...), custom_call_target="tpu_custom_call" | custom-call | flops 1 | bytes 1 | tf_op jit(solution)/shard_map/second/pallas_call | solution.py:440
  162.2 4.6 %collective-permute-start.11 = (f32[48,96]{1,0:T(8,128)S(1)}, f32[48,96]{1,0:T(8,128)S(1)}, u32[]{:S(2)}, u32[]{:S(2)}) collective-permute-start(f32[48,96]{1,0:T(8,128)S(1)} %get-tuple-element.26), channel_id=1, source_target_pairs={{0,5},{1,4},{2,15},{3,14},{4,9},{5,8},{6,3},{7,2},{8,13},{9,12},{1... | collective-permute-start | bytes 55304 | tf_op jit(solution)/shard_map/ppermute | solution.py:55
  166.8 1.8 %collective-permute-start.8 = (f32[48,96]{1,0:T(8,128)S(1)}, f32[48,96]{1,0:T(8,128)S(1)}, u32[]{:S(2)}, u32[]{:S(2)}) collective-permute-start(f32[48,96]{1,0:T(8,128)S(1)} %get-tuple-element.23), channel_id=1, source_target_pairs={{0,2},{1,3},{2,0},{3,1},{4,6},{5,7},{6,4},{7,5},{8,10},{9,11},{10,... | collective-permute-start | bytes 55304 | tf_op jit(solution)/shard_map/ppermute | solution.py:55
  168.7 2.7 %collective-permute-done.11 = f32[48,96]{1,0:T(8,128)S(1)} collective-permute-done((f32[48,96]{1,0:T(8,128)S(1)}, f32[48,96]{1,0:T(8,128)S(1)}, u32[]{:S(2)}, u32[]{:S(2)}) %collective-permute-start.11) | collective-permute-done | bytes 18464 | tf_op jit(solution)/shard_map/ppermute | solution.py:55
  171.4 0.6 collective-permute-done.9
  172.0 0.6 add_bitcast_fusion
  (19 shorter events, 1.7 us)
Async XLA Ops:
  21.5 92.1 %collective-permute-start = (bf16[784,3584]{1,0:T(8,128)(2,1)}, bf16[784,3584]{1,0:T(8,128)(2,1)}, u32[]{:S(2)}, u32[]{:S(2)}) collective-permute-start(bf16[784,3584]{1,0:T(8,128)(2,1)} %half.1), channel_id=1, source_target_pairs={{0,1},{1,0},{2,3},{3,2},{4,5},{5,4},{6,7},{7,6},{8,9},{9,8},{10,11... | collective-permute-start | bytes 16859144 | tf_op jit(solution)/shard_map/ppermute | solution.py:55
  22.0 81.8 %collective-permute-start.1 = (bf16[784,2304]{1,0:T(8,128)(2,1)}, bf16[784,2304]{1,0:T(8,128)(2,1)}, u32[]{:S(2)}, u32[]{:S(2)}) collective-permute-start(bf16[784,2304]{1,0:T(8,128)(2,1)} %get-tuple-element.17), channel_id=1, source_target_pairs={{0,2},{1,3},{2,0},{3,1},{4,6},{5,7},{6,4},{7,5},{8,10},{9,11},{10,... | collective-permute-start | bytes 10838024 | tf_op jit(solution)/shard_map/ppermute | solution.py:55
  24.5 82.4 %collective-permute-start.2 = (bf16[784,2304]{1,0:T(8,128)(2,1)}, bf16[784,2304]{1,0:T(8,128)(2,1)}, u32[]{:S(2)}, u32[]{:S(2)}) collective-permute-start(bf16[784,2304]{1,0:T(8,128)(2,1)} %get-tuple-element.16.xs), channel_id=1, source_target_pairs={{0,12},{1,13},{2,6},{3,7},{4,0},{5,1},{6,10},{7,11},{8,4},{9,5},{1... | collective-permute-start | bytes 10838024 | tf_op jit(solution)/shard_map/ppermute | solution.py:55
  36.2 110.2 %collective-permute-start.5 = (bf16[784,1280]{1,0:T(8,128)(2,1)}, bf16[784,1280]{1,0:T(8,128)(2,1)}, u32[]{:S(2)}, u32[]{:S(2)}) collective-permute-start(bf16[784,1280]{1,0:T(8,128)(2,1)} %get-tuple-element.19), channel_id=1, source_target_pairs={{0,3},{1,2},{2,1},{3,0},{4,7},{5,6},{6,5},{7,4},{8,11},{9,10},{10,... | collective-permute-start | bytes 6021128 | tf_op jit(solution)/shard_map/ppermute | solution.py:55
  36.2 113.0 %collective-permute-start.6 = (bf16[784,1280]{1,0:T(8,128)(2,1)}, bf16[784,1280]{1,0:T(8,128)(2,1)}, u32[]{:S(2)}, u32[]{:S(2)}) collective-permute-start(bf16[784,1280]{1,0:T(8,128)(2,1)} %get-tuple-element.20), channel_id=1, source_target_pairs={{0,13},{1,12},{2,7},{3,6},{4,1},{5,0},{6,11},{7,10},{8,5},{9,4},{1... | collective-permute-start | bytes 6021128 | tf_op jit(solution)/shard_map/ppermute | solution.py:55
  106.5 7.1 %copy-start = (bf16[768,1024]{1,0:T(8,128)(2,1)S(1)}, bf16[768,1024]{1,0:T(8,128)(2,1)}, u32[]{:S(2)}) copy-start(bf16[768,1024]{1,0:T(8,128)(2,1)} %grads.5) | copy-start | bytes 4718596
  106.5 3.7 %collective-permute-start.3 = (bf16[784,1024]{1,0:T(8,128)(2,1)}, bf16[784,1024]{1,0:T(8,128)(2,1)S(1)}, u32[]{:S(2)}, u32[]{:S(2)}) collective-permute-start(bf16[784,1024]{1,0:T(8,128)(2,1)} %slice.8), channel_id=1, source_target_pairs={{0,1},{1,0},{2,3},{3,2},{4,5},{5,4},{6,7},{7,6},{8,9},{9,8},{10,11... | collective-permute-start | bytes 4816904 | tf_op jit(solution)/shard_map/ppermute | solution.py:55
  109.8 3.8 %collective-permute-start.4 = (bf16[784,1024]{1,0:T(8,128)(2,1)}, bf16[784,1024]{1,0:T(8,128)(2,1)}, u32[]{:S(2)}, u32[]{:S(2)}) collective-permute-start(bf16[784,1024]{1,0:T(8,128)(2,1)} %slice.9), channel_id=1, source_target_pairs={{0,1},{1,0},{2,3},{3,2},{4,5},{5,4},{6,7},{7,6},{8,9},{9,8},{10,11... | collective-permute-start | bytes 4816904 | tf_op jit(solution)/shard_map/ppermute | solution.py:55
  162.2 6.5 %collective-permute-start.10 = (f32[48,96]{1,0:T(8,128)S(1)}, f32[48,96]{1,0:T(8,128)S(1)}, u32[]{:S(2)}, u32[]{:S(2)}) collective-permute-start(f32[48,96]{1,0:T(8,128)S(1)} %get-tuple-element.25), channel_id=1, source_target_pairs={{0,4},{1,5},{2,14},{3,15},{4,8},{5,9},{6,2},{7,3},{8,12},{9,13},{1... | collective-permute-start | bytes 55304 | tf_op jit(solution)/shard_map/ppermute | solution.py:55
  162.2 9.2 %collective-permute-start.11 = (f32[48,96]{1,0:T(8,128)S(1)}, f32[48,96]{1,0:T(8,128)S(1)}, u32[]{:S(2)}, u32[]{:S(2)}) collective-permute-start(f32[48,96]{1,0:T(8,128)S(1)} %get-tuple-element.26), channel_id=1, source_target_pairs={{0,5},{1,4},{2,15},{3,14},{4,9},{5,8},{6,3},{7,2},{8,13},{9,12},{1... | collective-permute-start | bytes 55304 | tf_op jit(solution)/shard_map/ppermute | solution.py:55
  166.8 4.6 %collective-permute-start.7 = (f32[48,96]{1,0:T(8,128)S(1)}, f32[48,96]{1,0:T(8,128)S(1)}, u32[]{:S(2)}, u32[]{:S(2)}) collective-permute-start(f32[48,96]{1,0:T(8,128)S(1)} %get-tuple-element.22), channel_id=1, source_target_pairs={{0,1},{1,0},{2,3},{3,2},{4,5},{5,4},{6,7},{7,6},{8,9},{9,8},{10,11... | collective-permute-start | bytes 55304 | tf_op jit(solution)/shard_map/ppermute | solution.py:55
  166.8 4.6 %collective-permute-start.8 = (f32[48,96]{1,0:T(8,128)S(1)}, f32[48,96]{1,0:T(8,128)S(1)}, u32[]{:S(2)}, u32[]{:S(2)}) collective-permute-start(f32[48,96]{1,0:T(8,128)S(1)} %get-tuple-element.23), channel_id=1, source_target_pairs={{0,2},{1,3},{2,0},{3,1},{4,6},{5,7},{6,4},{7,5},{8,10},{9,11},{10,... | collective-permute-start | bytes 55304 | tf_op jit(solution)/shard_map/ppermute | solution.py:55
  168.6 3.4 %collective-permute-start.9 = (f32[48,96]{1,0:T(8,128)S(1)}, f32[48,96]{1,0:T(8,128)S(1)}, u32[]{:S(2)}, u32[]{:S(2)}) collective-permute-start(f32[48,96]{1,0:T(8,128)S(1)} %get-tuple-element.24), channel_id=1, source_target_pairs={{0,3},{1,2},{2,1},{3,0},{4,7},{5,6},{6,5},{7,4},{8,11},{9,10},{10,... | collective-permute-start | bytes 55304 | tf_op jit(solution)/shard_map/ppermute | solution.py:55
